TPU v7x, 128 devices: a whole 4x4x4 slice. The times are simulated.
128 devices in a mesh: slab: 8 (over y, core), inner: 16 (over z, x).
Axes of the slice: x: 4, y: 4, z: 4, core: 2. Of those that a mesh axis runs over, the one named last changes fastest.
Arguments:
- x_in: bfloat16 [32768, 16384], P(('slab', 'inner')), may hold values from -6 to 6
- bc_in: bfloat16 [32768, 4096], P(('slab', 'inner')), may hold values from -6 to 6
- dt_raw: bfloat16 [32768, 256], P(('slab', 'inner')), may hold values from -6.7 to -4.3
- dt_bias: float32 [256], replicated, may hold values from -0.5 to 0.5
- a_log: float32 [256], replicated, may hold values from -8 to 0, as said below
- d_skip: float32 [256], replicated, may hold values from 0.5 to 1.5
- conv_x_weight: float32 [4, 16384], replicated, may hold values from -3 to 3
- conv_x_bias: float32 [16384], replicated, may hold values from -3 to 3
- conv_bc_weight: float32 [4, 4096], replicated, may hold values from -3 to 3
- conv_bc_bias: float32 [4096], replicated, may hold values from -3 to 3
Outputs:
- y_out: bfloat16 [32768, 16384], P('slab', 'inner')
Inputs may be any that keep to these rules, and one draw needn't show every extreme that they name: `a_log`: per-head logarithm of the decay rate.
All inputs are finite; a program needn't handle non-finite values.
Results may differ from a plain program's by a relative error of at most 0.0034.
Values may be sent and summed in bfloat16 or wider, within the bound.
A program may use at most 256 MiB of HBM per device.

v0:
```python
import jax
import jax.numpy as jnp
import numpy as np
from jax import lax
from jax.sharding import PartitionSpec as P

HEADS = 256
HEADDIM = 64
STATE = 256
GROUPS = 8
CONV = 4
SPAN = 256


def from_behind(x, axis, by):
    size = lax.axis_size(axis)
    pairs = [(i, i + by) for i in range(size) if 0 <= i + by < size]
    return lax.ppermute(x, axis, pairs)


def causal_conv(row_block, before, weight, conv_bias):
    kernel_len = weight.shape[0]
    length = row_block.shape[0]
    padded = jnp.concatenate([before, row_block], axis=0).astype(jnp.float32)
    summed = conv_bias[None, :] + weight[0][None, :] * padded[0:length]
    for offset in range(1, kernel_len):
        summed = summed + weight[offset][None, :] * padded[offset : offset + length]
    return jax.nn.silu(summed).astype(jnp.bfloat16)


def head_columns(per_head, head_count):
    rows = per_head.shape[0]
    return jnp.broadcast_to(per_head[:, :, None], (rows, head_count, HEADDIM)).reshape(
        rows, head_count * HEADDIM
    )


def span_step(state, pieces):
    x_span, b_span, c_span, dt_span, da_span = pieces
    size_q = x_span.shape[0]
    head_count = dt_span.shape[1]
    cumul = jnp.cumsum(da_span, axis=0).T
    row_ids = lax.broadcasted_iota(jnp.int32, (size_q, size_q), 0)
    col_ids = lax.broadcasted_iota(jnp.int32, (size_q, size_q), 1)
    gaps = cumul[:, :, None] - cumul[:, None, :]
    decays = jnp.where((row_ids >= col_ids)[None], jnp.exp(jnp.minimum(gaps, 0.0)), 0.0)
    scores = jnp.dot(c_span, b_span.T, preferred_element_type=jnp.float32)
    mixing = (decays * scores[None] * dt_span.T[:, None, :]).astype(jnp.bfloat16)
    x_heads = x_span.reshape(size_q, head_count, HEADDIM)
    y_intra = jnp.einsum(
        "hts,shp->thp", mixing, x_heads, preferred_element_type=jnp.float32
    ).reshape(size_q, head_count * HEADDIM)
    y_inter = jnp.dot(c_span, state.astype(jnp.bfloat16), preferred_element_type=jnp.float32)
    y_inter = y_inter * head_columns(jnp.exp(cumul.T), head_count)
    weights_end = (jnp.exp(cumul[:, -1:] - cumul) * dt_span.T).T
    scaled = (x_span.astype(jnp.float32) * head_columns(weights_end, head_count)).astype(
        jnp.bfloat16
    )
    contrib = jnp.dot(b_span.T, scaled, preferred_element_type=jnp.float32)
    end_decay = head_columns(jnp.exp(cumul[:, -1])[None, :], head_count)
    new_state = end_decay * state + contrib
    return (new_state, y_intra + y_inter)


def slab_core(x_rows, b_rows, c_rows, dt_rows, da_rows):
    length = x_rows.shape[0]
    width = x_rows.shape[1]
    head_count = dt_rows.shape[1]
    span_count = length // SPAN
    inputs = (
        x_rows.reshape(span_count, SPAN, width),
        b_rows.reshape(span_count, SPAN, STATE),
        c_rows.reshape(span_count, SPAN, STATE),
        dt_rows.reshape(span_count, SPAN, head_count),
        da_rows.reshape(span_count, SPAN, head_count),
    )
    zero_state = jnp.zeros((STATE, width), jnp.float32)
    end_state, outputs = lax.scan(span_step, zero_state, inputs)
    return (outputs.reshape(length, width), end_state)


def group_copies(bc_rows, dest_group, n_inner):
    tok_rows = bc_rows.shape[0]
    split = bc_rows.reshape(tok_rows, 2, GROUPS, STATE)
    picked = jnp.take(split, dest_group, axis=2)
    return jnp.transpose(picked, (0, 2, 1, 3)).reshape(tok_rows, n_inner, 2 * STATE)


def shards(
    x_in,
    bc_in,
    dt_raw,
    dt_bias,
    a_log,
    d_skip,
    conv_x_weight,
    conv_x_bias,
    conv_bc_weight,
    conv_bc_bias,
):
    n_inner = lax.axis_size("inner")
    n_slab = lax.axis_size("slab")
    tok_dev = x_in.shape[0]
    heads_dev = HEADS // n_inner
    ch_dev = heads_dev * HEADDIM
    per_group = HEADS // GROUPS
    inner_idx = lax.axis_index("inner")
    dest_group = np.arange(n_inner) * heads_dev // per_group
    edge = CONV - 1
    dt_send = dt_raw.reshape(tok_dev, n_inner, heads_dev)
    x_prev, bc_prev = from_behind(
        (x_in[tok_dev - edge :], bc_in[tok_dev - edge :]), ("slab", "inner"), 1
    )
    x_ready = causal_conv(x_in, x_prev, conv_x_weight, conv_x_bias)
    bc_ready = causal_conv(bc_in, bc_prev, conv_bc_weight, conv_bc_bias)
    bc_send = group_copies(bc_ready, dest_group, n_inner)
    x_recv, bc_recv, dt_recv = (
        lax.all_to_all(
            x_ready.reshape(tok_dev, n_inner, ch_dev),
            "inner",
            split_axis=1,
            concat_axis=0,
            tiled=True,
        ),
        lax.all_to_all(bc_send, "inner", split_axis=1, concat_axis=0, tiled=True),
        lax.all_to_all(dt_send, "inner", split_axis=1, concat_axis=0, tiled=True),
    )
    x_slab = x_recv.reshape(-1, ch_dev)
    bc_slab = bc_recv.reshape(-1, 2 * STATE)
    bias_heads = lax.dynamic_slice_in_dim(dt_bias, inner_idx * heads_dev, heads_dev, 0)
    rate_heads = -jnp.exp(lax.dynamic_slice_in_dim(a_log, inner_idx * heads_dev, heads_dev, 0))
    skip_heads = lax.dynamic_slice_in_dim(d_skip, inner_idx * heads_dev, heads_dev, 0)
    dt_heads = jax.nn.softplus(
        dt_recv.reshape(-1, heads_dev).astype(jnp.float32) + bias_heads[None, :]
    )
    da_heads = dt_heads * rate_heads[None, :]
    c_slab = bc_slab[:, STATE:]
    y_local, end_state = slab_core(x_slab, bc_slab[:, :STATE], c_slab, dt_heads, da_heads)
    cum_slab = jnp.cumsum(da_heads, axis=0)
    slab_decay = head_columns(jnp.exp(cum_slab[-1:]), heads_dev)[0]
    incoming = jnp.zeros_like(end_state)
    outgoing = end_state
    for hop_number in range(n_slab - 1):
        incoming = from_behind(outgoing, "slab", 1)
        outgoing = slab_decay[None, :] * incoming + end_state
    carried = jnp.dot(c_slab, incoming.astype(jnp.bfloat16), preferred_element_type=jnp.float32)
    carried = carried * head_columns(jnp.exp(cum_slab), heads_dev)
    skip_cols = jnp.repeat(skip_heads, HEADDIM)
    y_slab = y_local + carried + skip_cols[None, :] * x_slab.astype(jnp.float32)
    return y_slab.astype(jnp.bfloat16)


def solution(mesh):
    placed = (
        P(("slab", "inner"), None),
        P(("slab", "inner"), None),
        P(("slab", "inner"), None),
        P(),
        P(),
        P(),
        P(),
        P(),
        P(),
        P(),
    )
    return jax.shard_map(
        shards, mesh=mesh, in_specs=placed, out_specs=P("slab", "inner"), check_vma=False
    )
```

profile of v0, /device:TPU:1, one launch (start us, length us, event | category | flops | bytes accessed | tf_op | source)
XLA Modules:
  0.0 632.0 jit_solution(11181549792575197285)
XLA Ops:
  1.6 8.4 %all-to-all-start = ((bf16[256,16,16]{0,2,1:T(8,128)(2,1)}), bf16[256,16,16]{0,2,1:T(8,128)(2,1)S(1)}, u32[]{:S(2)}, u32[]{:S(2)}) async-start(bf16[256,16,16]{0,2,1:T(8,128)(2,1)} %bitcast), calls=%async_computation | async-start | bytes 262144 | tf_op jit(solution)/shard_map/all_to_all | solution.py:126
  10.9 3.3 collective-permute-start
  15.9 3.1 collective-permute-start.1
  22.9 3.3 copy.85
  28.8 7.7 %multiply_convert_fusion.4 = bf16[256,4096]{0,1:T(8,128)(2,1)} fusion(f32[259,4096]{0,1:T(8,128)S(1)} %maximum_convert_fusion.1, f32[4096]{0:T(1024)S(1)} %bitcast.205, f32[4096]{0:T(1024)S(1)} %bitcast.206, f32[4096]{0:T(1024)S(1)} %bitcast.204, f32[4096]{0:T(1024)S(1)} %bitcast.203, f32[4096]{0:T(1024)S(1)} %copy-done.4), kind=kLoop, calls=%fused_computation.66 | loop fusion | flops 13631488 | bytes 18956288 | tf_op jit(solution)/shard_map/convert_element_type | solution.py:28
  36.5 2.9 copy.86
  39.3 2.8 gather_fusion
  42.1 6.4 %copy.87 = bf16[256,16,2,256]{0,3,2,1:T(8,128)(2,1)} copy(bf16[256,16,2,256]{3,0,2,1:T(8,128)(2,1)} %bitcast.192) | data formatting | bytes 8388608 | tf_op jit(solution)/shard_map/jit(_take)/select_n | solution.py:85
  48.5 11.8 %maximum_convert_fusion = f32[259,16384]{1,0:T(8,128)} fusion(bf16[256,16384]{1,0:T(8,128)(2,1)} %param.13, bf16[3,16384]{1,0:T(4,128)(2,1)} %collective-permute-done.1), kind=kLoop, calls=%fused_computation.56 | loop fusion | flops 16973824 | bytes 25460736 | tf_op jit(solution)/shard_map/convert_element_type | solution.py:24
  60.3 7.6 %all-to-all-start.1 = ((bf16[256,16,512]{0,2,1:T(8,128)(2,1)}), bf16[256,16,512]{0,2,1:T(8,128)(2,1)}, u32[]{:S(2)}, u32[]{:S(2)}) async-start(bf16[256,16,512]{0,2,1:T(8,128)(2,1)} %bitcast.191), calls=%async_computation.1 | async-start | bytes 8388608 | tf_op jit(solution)/shard_map/all_to_all | solution.py:125
  67.9 27.1 %multiply_convert_fusion.3 = bf16[256,16384]{1,0:T(8,128)(2,1)} fusion(f32[259,16384]{1,0:T(8,128)} %maximum_convert_fusion, f32[16384]{0:T(1024)S(1)} %bitcast.201, f32[16384]{0:T(1024)S(1)} %bitcast.202, f32[16384]{0:T(1024)S(1)} %bitcast.200, f32[16384]{0:T(1024)S(1)} %bitcast.199, f32[16384]{0:T(1024)S(1)} %copy-done.3), kind=kLoop, calls=%fused_computation.55 | loop fusion | flops 54525952 | bytes 75825152 | tf_op jit(solution)/shard_map/convert_element_type | solution.py:28
  95.0 12.0 %copy.89 = bf16[256,16384]{0,1:T(8,128)(2,1)} copy(bf16[256,16384]{1,0:T(8,128)(2,1)} %multiply_convert_fusion.3) | data formatting | bytes 16777216 | tf_op jit(solution)/shard_map/convert_element_type | solution.py:28
  107.0 23.8 %all-to-all-done.1 = bf16[256,16,512]{0,2,1:T(8,128)(2,1)} async-done(((bf16[256,16,512]{0,2,1:T(8,128)(2,1)}), bf16[256,16,512]{0,2,1:T(8,128)(2,1)}, u32[]{:S(2)}, u32[]{:S(2)}) %all-to-all-start.1) | async-done | bytes 4194336 | tf_op jit(solution)/shard_map/all_to_all | solution.py:125
  130.8 5.1 all-to-all-start.2
  137.1 6.4 %copy.88 = bf16[16,256,1,512]{3,1,0,2:T(8,128)(2,1)} copy(bf16[16,256,1,512]{1,3,0,2:T(8,128)(2,1)} %bitcast.12) | data formatting | bytes 8388608 | tf_op jit(solution)/shard_map/all_to_all | solution.py:125
  143.5 4.5 fusion.49
  148.1 109.2 %all-to-all-done.2 = bf16[256,16,1024]{0,2,1:T(8,128)(2,1)} async-done(((bf16[256,16,1024]{0,2,1:T(8,128)(2,1)}), bf16[256,16,1024]{0,2,1:T(8,128)(2,1)}, u32[]{:S(2)}, u32[]{:S(2)}) %all-to-all-start.2) | async-done | bytes 8388640 | tf_op jit(solution)/shard_map/all_to_all | solution.py:118
  257.2 209.6 %while.13 = (s32[]{:T(128)}, f32[256,1024]{1,0:T(8,128)S(1)}, f32[16,256,1024]{2,1,0:T(8,128)}, f32[16,256,16]{1,2,0:T(8,128)}, bf16[16,256,256]{2,1,0:T(8,128)(...) while((s32[]{:T(128)}, f32[256,1024]{1,0:T(8,128)S(1)}, ...), condition=%wide.region_3.4_spmd.clone, body=%wide.region_0.3_spmd.clone.sunk | while | flops 445460544 | bytes 21369472 | solution.py:78
  279.5 2.3 fusion.73
  292.7 2.3 fusion.73
  305.8 2.2 fusion.73
  318.8 2.2 fusion.73
  331.9 2.3 fusion.73
  345.0 2.3 fusion.73
  358.1 2.3 fusion.73
  371.2 2.3 fusion.73
  410.5 2.3 fusion.73
  423.6 2.3 fusion.73
  436.8 2.3 fusion.73
  449.8 2.3 fusion.73
  463.0 2.3 fusion.73
  466.8 5.6 collective-permute-start.2
  472.8 4.6 reduce-window.16
  478.5 5.7 collective-permute-done.2
  484.3 4.4 collective-permute-start.3
  488.7 11.7 %collective-permute-done.3 = f32[256,1024]{1,0:T(8,128)S(1)} collective-permute-done((f32[256,1024]{1,0:T(8,128)S(1)}, f32[256,1024]{1,0:T(8,128)S(1)}, u32[]{:S(2)}, u32[]{:S(2)}) %collective-permute-start.3) | collective-permute-done | bytes 1048608 | tf_op jit(solution)/shard_map/ppermute | solution.py:18
  500.7 4.4 collective-permute-start.4
  505.1 11.7 %collective-permute-done.4 = f32[256,1024]{1,0:T(8,128)S(1)} collective-permute-done((f32[256,1024]{1,0:T(8,128)S(1)}, f32[256,1024]{1,0:T(8,128)S(1)}, u32[]{:S(2)}, u32[]{:S(2)}) %collective-permute-start.4) | collective-permute-done | bytes 1048608 | tf_op jit(solution)/shard_map/ppermute | solution.py:18
  517.0 4.4 collective-permute-start.5
  521.4 11.7 %collective-permute-done.5 = f32[256,1024]{1,0:T(8,128)S(1)} collective-permute-done((f32[256,1024]{1,0:T(8,128)S(1)}, f32[256,1024]{1,0:T(8,128)S(1)}, u32[]{:S(2)}, u32[]{:S(2)}) %collective-permute-start.5) | collective-permute-done | bytes 1048608 | tf_op jit(solution)/shard_map/ppermute | solution.py:18
  533.3 4.4 collective-permute-start.6
  537.7 11.7 %collective-permute-done.6 = f32[256,1024]{1,0:T(8,128)S(1)} collective-permute-done((f32[256,1024]{1,0:T(8,128)S(1)}, f32[256,1024]{1,0:T(8,128)S(1)}, u32[]{:S(2)}, u32[]{:S(2)}) %collective-permute-start.6) | collective-permute-done | bytes 1048608 | tf_op jit(solution)/shard_map/ppermute | solution.py:18
  550.5 4.4 collective-permute-start.7
  555.3 7.8 %broadcast_in_dim.88 = f32[4096,16,64]{0,2,1:T(8,128)} broadcast(f32[4096,16]{0,1:T(8,128)S(1)} %fusion.47), dimensions={0,1} | broadcast | bytes 17039360 | tf_op jit(solution)/shard_map/broadcast_in_dim | solution.py:33
  563.1 17.5 %copy.91 = f32[4096,1024]{1,0:T(8,128)} copy(f32[4096,1024]{0,1:T(8,128)} %bitcast.183) | data formatting | bytes 33554432 | tf_op jit(solution)/shard_map/reshape | solution.py:33
  582.7 10.9 %bitcast_convert_fusion = f32[16,256,1,1024]{1,3,0,2:T(8,128)} fusion(bf16[256,16,1024]{0,2,1:T(8,128)(2,1)} %all-to-all-done.2), kind=kLoop, calls=%fused_computation.57 | loop fusion | flops 4194304 | bytes 25165824 | tf_op jit(solution)/shard_map/convert_element_type | solution.py:149
  593.6 17.6 %copy.92 = f32[16,256,1,1024]{3,1,0,2:T(8,128)} copy(f32[16,256,1,1024]{1,3,0,2:T(8,128)} %bitcast_convert_fusion) | data formatting | bytes 33554432 | tf_op jit(solution)/shard_map/convert_element_type | solution.py:149
  611.2 20.8 %fusion.31 = bf16[4096,1024]{1,0:T(8,128)(2,1)} fusion(f32[16,256,1,1024]{3,1,0,2:T(8,128)} %copy.92, f32[16,256,1024]{2,1,0:T(8,128)} %get-tuple-element.48, f32[4096,1024]{1,0:T(8,128)} %copy.91, f32[1024]{0:T(1024)S(1)} %mul.236, bf16[256,1024]{1,0:T(8,128)(2,1)S(1)} %collective-permute-done.8, bf16[4096,512]{1,0:T(8,128)(2,1)} %bitcast.189), kind=kOutput, calls=%fused_computation.53 | convolution fusion | flops 2168455168 | bytes 61345792 | tf_op jit(solution)/shard_map/dot_general | solution.py:146
  (439 shorter events, 196.0 us)
Async XLA Ops:
  1.6 58.6 %all-to-all-start = ((bf16[256,16,16]{0,2,1:T(8,128)(2,1)}), bf16[256,16,16]{0,2,1:T(8,128)(2,1)S(1)}, u32[]{:S(2)}, u32[]{:S(2)}) async-start(bf16[256,16,16]{0,2,1:T(8,128)(2,1)} %bitcast), calls=%async_computation | async-start | bytes 262144 | tf_op jit(solution)/shard_map/all_to_all | solution.py:126
  10.9 15.2 %collective-permute-start = (bf16[3,4096]{1,0:T(4,128)(2,1)S(1)}, bf16[3,4096]{1,0:T(4,128)(2,1)}, u32[]{:S(2)}, u32[]{:S(2)}) collective-permute-start(bf16[3,4096]{1,0:T(4,128)(2,1)S(1)} %slice.80), channel_id=1, source_target_pairs={{0,1},{1,2},{2,3},{3,4},{4,5},{5,6},{6,7},{7,8},{8,9},{9,10},{10,1... | collective-permute-start | bytes 73736 | tf_op jit(solution)/shard_map/ppermute | solution.py:18
  15.9 32.6 %collective-permute-start.1 = (bf16[3,16384]{1,0:T(4,128)(2,1)}, bf16[3,16384]{1,0:T(4,128)(2,1)}, u32[]{:S(2)}, u32[]{:S(2)}) collective-permute-start(bf16[3,16384]{1,0:T(4,128)(2,1)} %slice.90), channel_id=1, source_target_pairs={{0,1},{1,2},{2,3},{3,4},{4,5},{5,6},{6,7},{7,8},{8,9},{9,10},{10,1... | collective-permute-start | bytes 294920 | tf_op jit(solution)/shard_map/ppermute | solution.py:18
  60.3 7.6 %copy-start.2 = (f32[1,16384]{1,0:T(1,128)S(1)}, f32[1,16384]{1,0:T(1,128)}, u32[]{:S(2)}) copy-start(f32[1,16384]{1,0:T(1,128)} %get-tuple-element.109) | copy-start | bytes 196612
  60.3 7.6 %copy-start.3 = (f32[16384]{0:T(1024)S(1)}, f32[16384]{0:T(1024)}, u32[]{:S(2)}) copy-start(f32[16384]{0:T(1024)} %param.20) | copy-start | bytes 196612
  60.3 70.5 %all-to-all-start.1 = ((bf16[256,16,512]{0,2,1:T(8,128)(2,1)}), bf16[256,16,512]{0,2,1:T(8,128)(2,1)}, u32[]{:S(2)}, u32[]{:S(2)}) async-start(bf16[256,16,512]{0,2,1:T(8,128)(2,1)} %bitcast.191), calls=%async_computation.1 | async-start | bytes 8388608 | tf_op jit(solution)/shard_map/all_to_all | solution.py:125
  130.8 5.1 copy-start.5
  130.8 5.2 copy-start.6
  130.8 126.5 %all-to-all-start.2 = ((bf16[256,16,1024]{0,2,1:T(8,128)(2,1)}), bf16[256,16,1024]{0,2,1:T(8,128)(2,1)}, u32[]{:S(2)}, u32[]{:S(2)}) async-start(bf16[256,16,1024]{0,2,1:T(8,128)(2,1)} %bitcast.187), calls=%async_computation.2 | async-start | bytes 16777216 | tf_op jit(solution)/shard_map/all_to_all | solution.py:118
  262.1 1.4 copy-start
  266.4 2.3 copy-start.1
  275.1 1.4 copy-start
  279.5 2.3 copy-start.1
  288.3 1.4 copy-start
  292.6 2.3 copy-start.1
  301.4 1.4 copy-start
  305.7 2.3 copy-start.1
  314.4 1.4 copy-start
  318.8 2.3 copy-start.1
  327.5 1.4 copy-start
  331.9 2.3 copy-start.1
  340.6 1.4 copy-start
  345.0 2.3 copy-start.1
  353.7 1.4 copy-start
  358.1 2.3 copy-start.1
  366.9 1.4 copy-start
  371.2 2.3 copy-start.1
  380.0 1.4 copy-start
  384.4 2.2 copy-start.1
  393.1 1.4 copy-start
  397.4 2.3 copy-start.1
  406.1 1.4 copy-start
  410.5 2.3 copy-start.1
  419.2 1.4 copy-start
  423.6 2.3 copy-start.1
  432.4 1.4 copy-start
  436.7 2.3 copy-start.1
  449.8 2.3 copy-start.1
  458.6 1.4 copy-start
  462.9 2.3 copy-start.1
  466.8 17.4 %collective-permute-start.2 = (f32[256,1024]{1,0:T(8,128)S(1)}, f32[256,1024]{1,0:T(8,128)S(1)}, u32[]{:S(2)}, u32[]{:S(2)}) collective-permute-start(f32[256,1024]{1,0:T(8,128)S(1)} %get-tuple-element.49), channel_id=1, source_target_pairs={{0,16},{16,32},{32,48},{48,64},{64,80},{80,96},{96,112},{1,17},{17... | collective-permute-start | bytes 3145736 | tf_op jit(solution)/shard_map/ppermute | solution.py:18
  484.3 16.1 %collective-permute-start.3 = (f32[256,1024]{1,0:T(8,128)S(1)}, f32[256,1024]{1,0:T(8,128)S(1)}, u32[]{:S(2)}, u32[]{:S(2)}) collective-permute-start(f32[256,1024]{1,0:T(8,128)S(1)} %multiply_add_fusion.5), channel_id=1, source_target_pairs={{0,16},{16,32},{32,48},{48,64},{64,80},{80,96},{96,112},{1,17},{17... | collective-permute-start | bytes 3145736 | tf_op jit(solution)/shard_map/ppermute | solution.py:18
  500.6 54.3 %copy-start.7 = (f32[256]{0:T(256)S(1)}, f32[256]{0:T(256)}, u32[]{:S(2)}) copy-start(f32[256]{0:T(256)} %param.18) | copy-start | bytes 3076
  500.7 16.1 %collective-permute-start.4 = (f32[256,1024]{1,0:T(8,128)S(1)}, f32[256,1024]{1,0:T(8,128)S(1)}, u32[]{:S(2)}, u32[]{:S(2)}) collective-permute-start(f32[256,1024]{1,0:T(8,128)S(1)} %multiply_add_fusion.4), channel_id=1, source_target_pairs={{0,16},{16,32},{32,48},{48,64},{64,80},{80,96},{96,112},{1,17},{17... | collective-permute-start | bytes 3145736 | tf_op jit(solution)/shard_map/ppermute | solution.py:18
  517.0 16.1 %collective-permute-start.5 = (f32[256,1024]{1,0:T(8,128)S(1)}, f32[256,1024]{1,0:T(8,128)S(1)}, u32[]{:S(2)}, u32[]{:S(2)}) collective-permute-start(f32[256,1024]{1,0:T(8,128)S(1)} %multiply_add_fusion.3), channel_id=1, source_target_pairs={{0,16},{16,32},{32,48},{48,64},{64,80},{80,96},{96,112},{1,17},{17... | collective-permute-start | bytes 3145736 | tf_op jit(solution)/shard_map/ppermute | solution.py:18
  533.3 16.1 %collective-permute-start.6 = (f32[256,1024]{1,0:T(8,128)S(1)}, f32[256,1024]{1,0:T(8,128)S(1)}, u32[]{:S(2)}, u32[]{:S(2)}) collective-permute-start(f32[256,1024]{1,0:T(8,128)S(1)} %multiply_add_fusion.2), channel_id=1, source_target_pairs={{0,16},{16,32},{32,48},{48,64},{64,80},{80,96},{96,112},{1,17},{17... | collective-permute-start | bytes 3145736 | tf_op jit(solution)/shard_map/ppermute | solution.py:18
  550.5 30.0 %collective-permute-start.7 = (f32[256,1024]{1,0:T(8,128)}, f32[256,1024]{1,0:T(8,128)S(1)}, u32[]{:S(2)}, u32[]{:S(2)}) collective-permute-start(f32[256,1024]{1,0:T(8,128)} %multiply_add_fusion.1), channel_id=1, source_target_pairs={{0,16},{16,32},{32,48},{48,64},{64,80},{80,96},{96,112},{1,17},{17... | collective-permute-start | bytes 3145736 | tf_op jit(solution)/shard_map/ppermute | solution.py:18
  580.8 30.4 %collective-permute-start.8 = (bf16[256,1024]{1,0:T(8,128)(2,1)S(1)}, bf16[256,1024]{1,0:T(8,128)(2,1)S(1)}, u32[]{:S(2)}, u32[]{:S(2)}) collective-permute-start(bf16[256,1024]{1,0:T(8,128)(2,1)S(1)} %multiply_add_fusion), channel_id=1, source_target_pairs={{0,16},{16,32},{32,48},{48,64},{64,80},{80,96},{96,112},{1,17},{17... | collective-permute-start | bytes 1572872 | tf_op jit(solution)/shard_map/ppermute | solution.py:18
  (2 other events, 2.7 us)
where the time goes:
time: 638 us; the launch traced here: 632 us
  waiting for transfers between devices  185 us (29%)
  local copies, waits for them, and re-layouts  175 us (27%)
  matrix products  119 us (19%)
  other arithmetic  93.7 us (15%)
  starting transfers between devices  56.9 us (9%)
    all_to_all x1, waiting for transfers between devices, shards(): lax.all_to_all(x_ready.reshape(tok_dev, n_inner, ch_dev), 'inner', split_...  109 us
    ppermute x9, waiting for transfers between devices, from_behind(): return lax.ppermute(x, axis, pairs)  52.6 us
    reshape x17, local copies, waits for them, and re-layouts, head_columns(): jnp.broadcast_to(per_head[:, :, None], (rows, head_count, HEADDIM))  42.3 us
    dot_general x16, matrix products, span_step(): jnp.dot(c_span, state.astype(jnp.bfloat16), preferred_element_type=jnp.fl...  36.3 us
    ppermute x9, starting transfers between devices, from_behind(): return lax.ppermute(x, axis, pairs)  35.8 us
    convert_element_type x2, other arithmetic, causal_conv(): return jax.nn.silu(summed).astype(jnp.bfloat16)  34.8 us
    broadcast_in_dim x51, local copies, waits for them, and re-layouts, head_columns(): jnp.broadcast_to(per_head[:, :, None], (rows, head_count, HEADDIM))  27.2 us
    all_to_all x1, waiting for transfers between devices, shards(): lax.all_to_all(bc_send, 'inner', split_axis=1, concat_axis=0, tiled=True)  23.8 us
  transfers between devices with their start and end apart: 12, of which 7 were waited for; matrix products, arithmetic and copies ran while one was open for 25% of the time, Pallas kernels for 0%

commit v1 on v0

v1 whole, which is shorter than its diff:
```python
import jax
import jax.numpy as jnp
from jax import lax
from jax.experimental import pallas as pl
from jax.experimental.pallas import tpu as pltpu
from jax.sharding import PartitionSpec as P

HEADS = 256
HEADDIM = 64
STATE = 256
GROUPS = 8
SPAN = 256
N_SLAB = 8
N_INNER = 16
CH = 1024
NH = 16
PIECES = 4
COLS = CH // PIECES
EDGE = 16
SUB = 64
MESH = pl.DeviceIdType.MESH
ORDER = (
    (2, 2), (1, 0), (0, 3), (3, 1), (2, 1), (0, 1), (3, 0), (1, 3),
    (1, 2), (2, 0), (3, 3), (0, 2), (1, 1), (2, 3), (3, 2),
)
N_PEER = len(ORDER)
F32 = jnp.float32
BF16 = jnp.bfloat16


def dot(a, b):
    return jnp.dot(a, b, preferred_element_type=F32)


def conv_silu(rows, weight, bias):
    full = rows.astype(F32)
    n = rows.shape[0] - EDGE
    acc = bias
    for k in range(4):
        start = EDGE - 3 + k
        acc = acc + weight[k : k + 1, :] * full[start : start + n]
    half = 0.5 * acc
    return (half + half * jnp.tanh(half)).astype(BF16)


def body(
    x_ref, bc_ref, dt_ref, head_ref, wx_ref, bx_ref, wbc_ref, bbc_ref,
    out_ref,
    xbuf, bbuf, cbuf, dtbuf, dt_t, gm, cc, bt, coef, ew, ee, dec, ep, tot, skip, state, xs, xc, ebuf, arr, inc,
    xsend, xrecv, ssend, srecv, hsend, hrecv, tsend, trecv, esend, erecv, osem,
):
    slab = lax.axis_index("slab")
    me = lax.axis_index("inner")
    my_z, my_x = me // 4, lax.rem(me, 4)
    sign = 1 - 2 * lax.rem(slab, 2)
    peers = [
        lax.rem(my_z + sign * dz + 4, 4) * 4 + lax.rem(my_x + sign * dx + 4, 4)
        for dx, dz in ORDER
    ]
    halo_out = jnp.logical_and(me == N_INNER - 1, slab < N_SLAB - 1)

    barrier = pltpu.get_barrier_semaphore()
    for peer in peers:
        pl.semaphore_signal(barrier, inc=1, device_id=(slab, peer), device_id_type=MESH)
    for k in range(1, N_SLAB):

        @pl.when(slab >= k)
        def _():
            pl.semaphore_signal(barrier, inc=1, device_id=(slab - k, me), device_id_type=MESH)

    @pl.when(slab > 0)
    def _():
        pl.semaphore_signal(barrier, inc=1, device_id=(slab - 1, N_INNER - 1), device_id_type=MESH)

    pl.semaphore_wait(
        barrier, N_PEER + (N_SLAB - 1 - slab) + jnp.where(halo_out, N_INNER, 0)
    )

    def rows_of(j):
        return pl.ds(pl.multiple_of(EDGE + j * SPAN, EDGE), SPAN)

    def x_cols(d, p):
        return pl.ds(pl.multiple_of(d * CH + p * COLS, COLS), COLS)

    def bc_cols(d, which):
        return pl.ds(pl.multiple_of((d // 2 + which * GROUPS) * STATE, STATE), STATE)

    def remote(src, dst, send_sem, recv_sem, to):
        return pltpu.make_async_remote_copy(
            src, dst, send_sem, recv_sem, device_id=to, device_id_type=MESH
        )

    def bc_copy(n, which):
        buf = (bbuf, cbuf)[which]
        return remote(
            bc_ref.at[:, bc_cols(peers[n], which)], buf.at[rows_of(me)],
            ssend.at[which, n], srecv.at[which, me], (slab, peers[n]),
        )

    def dt_copy(n):
        return remote(
            dt_t.at[pl.ds(pl.multiple_of(peers[n] * NH, NH), NH)], dtbuf.at[me],
            ssend.at[2, n], srecv.at[2, me], (slab, peers[n]),
        )

    def x_copy(n, p):
        return remote(
            x_ref.at[:, x_cols(peers[n], p)], xbuf.at[p, rows_of(me)],
            xsend.at[p, n], xrecv.at[p, me], (slab, peers[n]),
        )

    def halo_copies(d):
        tail = pl.ds(SPAN - EDGE, EDGE)
        to = (slab + 1, d)
        return [
            remote(bc_ref.at[tail, bc_cols(d, 0)], bbuf.at[pl.ds(0, EDGE)], hsend.at[0, d], hrecv.at[0], to),
            remote(bc_ref.at[tail, bc_cols(d, 1)], cbuf.at[pl.ds(0, EDGE)], hsend.at[1, d], hrecv.at[1], to),
        ] + [
            remote(
                x_ref.at[tail, x_cols(d, p)], xbuf.at[p, pl.ds(0, EDGE)], hsend.at[2 + p, d], hrecv.at[2 + p], to
            )
            for p in range(PIECES)
        ]

    dt_t[...] = dt_ref[...].astype(F32).T.astype(BF16)
    for n in range(N_PEER):
        dt_copy(n).start()
    for n in range(N_PEER):
        for which in range(2):
            bc_copy(n, which).start()

    @pl.when(halo_out)
    def _():
        @pl.loop(0, N_INNER)
        def _(d):
            for copy in halo_copies(d):
                copy.start()

    own = [
        pltpu.make_async_copy(bc_ref.at[:, bc_cols(me, 0)], bbuf.at[rows_of(me)], srecv.at[0, me]),
        pltpu.make_async_copy(bc_ref.at[:, bc_cols(me, 1)], cbuf.at[rows_of(me)], srecv.at[1, me]),
        pltpu.make_async_copy(
            dt_t.at[pl.ds(pl.multiple_of(me * NH, NH), NH)], dtbuf.at[me], srecv.at[2, me]
        ),
    ] + [
        pltpu.make_async_copy(x_ref.at[:, x_cols(me, p)], xbuf.at[p, rows_of(me)], xrecv.at[p, me])
        for p in range(PIECES)
    ]
    for copy in own:
        copy.start()
    for p in range(PIECES):
        for n in range(N_PEER):
            x_copy(n, p).start()

    chan = lax.broadcasted_iota(jnp.int32, (128, CH), 1) // HEADDIM
    row = lax.broadcasted_iota(jnp.int32, (128, CH), 0)
    ew[...] = jnp.where((row < 2 * NH) & (lax.rem(row, NH) == chan), 1.0, 0.0).astype(BF16)
    ee[...] = jnp.where(
        (row >= 2 * NH) & (row < 4 * NH) & (lax.rem(row, NH) == chan), 1.0, 0.0
    ).astype(BF16)
    heads = head_ref[pl.ds(pl.multiple_of(me * NH, NH), NH), :]
    bias_col, rate_col, skip_col = heads[:, 0:1], -jnp.exp(heads[:, 1:2]), heads[:, 2:3]
    pick = lax.broadcasted_iota(jnp.int32, (NH, CH), 0) == (
        lax.broadcasted_iota(jnp.int32, (NH, CH), 1) // HEADDIM
    )
    skip[...] = jnp.sum(jnp.where(pick, skip_col, 0.0), axis=0, keepdims=True)
    ep[0] = jnp.ones((1, CH), F32)
    row_ids = lax.broadcasted_iota(jnp.int32, (SPAN, SPAN), 0)
    col_ids = lax.broadcasted_iota(jnp.int32, (SPAN, SPAN), 1)
    upto = jnp.where(row_ids <= col_ids, 1.0, 0.0).astype(F32)

    @pl.when(slab == 0)
    def _():
        bbuf[pl.ds(0, EDGE), :] = jnp.zeros((EDGE, STATE), BF16)
        cbuf[pl.ds(0, EDGE), :] = jnp.zeros((EDGE, STATE), BF16)
        for p in range(PIECES):
            xbuf[p, pl.ds(0, EDGE), :] = jnp.zeros((EDGE, COLS), BF16)

    @pl.when(slab > 0)
    def _():
        for k, buf in enumerate((bbuf, cbuf)):
            edge = buf.at[pl.ds(0, EDGE)]
            pltpu.make_async_copy(edge, edge, hrecv.at[k]).wait()
        for p in range(PIECES):
            edge = xbuf.at[p, pl.ds(0, EDGE)]
            pltpu.make_async_copy(edge, edge, hrecv.at[2 + p]).wait()

    b_at = bc_cols(me, 0)
    c_at = bc_cols(me, 1)

    @pl.loop(0, N_INNER)
    def _(j):
        slot = dtbuf.at[j]
        pltpu.make_async_copy(slot, slot, srecv.at[2, j]).wait()
        raw = dtbuf[j].astype(F32) + bias_col
        dt = jnp.maximum(raw, 0.0) + jnp.log1p(jnp.exp(-jnp.abs(raw)))
        da = dt * rate_col
        cumul = jnp.dot(da, upto, preferred_element_type=F32, precision=lax.Precision.HIGHEST)
        grow = jnp.exp(-cumul) * dt
        decay = jnp.exp(cumul)
        grow_hi = grow.astype(BF16).astype(F32)
        decay_hi = decay.astype(BF16).astype(F32)
        parts = jnp.concatenate(
            [grow_hi, grow - grow_hi, decay_hi, decay - decay_hi, jnp.zeros((4 * NH, SPAN), F32)],
            axis=0,
        )
        at = pl.ds(pl.multiple_of(j * SPAN, SPAN), SPAN)
        coef_j = parts.T.astype(BF16)
        coef[at, :] = coef_j
        dec_j = dot(coef_j[SPAN - EDGE :], ee[...])[EDGE - 1 : EDGE]
        dec[j] = dec_j
        ep[j + 1] = ep[j] * dec_j

        for k, buf in enumerate((bbuf, cbuf)):
            slot = buf.at[rows_of(j)]
            pltpu.make_async_copy(slot, slot, srecv.at[k, j]).wait()

        def conv_of(buf, cols):
            weight, bias = wbc_ref[:, cols], bbc_ref[:, cols]
            return jnp.concatenate(
                [
                    conv_silu(
                        buf[pl.ds(pl.multiple_of(j * SPAN + r, EDGE), SUB + EDGE), :], weight, bias
                    )
                    for r in range(0, SPAN, SUB)
                ],
                axis=0,
            )

        b_j = conv_of(bbuf, b_at)
        c_j = conv_of(cbuf, c_at)
        cc[at, :] = c_j
        b_t = b_j.astype(F32).T.astype(BF16)
        bt[at, :] = b_t
        gm[at, :] = jnp.where(row_ids >= col_ids, dot(c_j, b_t), 0.0).astype(BF16)

    def tot_copy(k):
        return remote(ep.at[N_INNER], tot.at[slab], tsend.at[k], trecv.at[slab], (slab + k, me))

    for k in range(1, N_SLAB):

        @pl.when(slab + k < N_SLAB)
        def _():
            tot_copy(k).start()

    @pl.loop(0, slab)
    def _(m):
        slot = tot.at[m]
        pltpu.make_async_copy(slot, slot, trecv.at[m]).wait()

    def end_copy(p, k):
        return remote(
            ebuf.at[p], arr.at[p, slab], esend.at[p, k], erecv.at[p, slab], (slab + k, me)
        )

    def out_copy(p, j):
        at = pl.ds(pl.multiple_of(j * SPAN, SPAN), SPAN)
        return pltpu.make_async_copy(
            xc.at[p % 2, at], out_ref.at[at, pl.ds(p * COLS, COLS)], osem.at[p % 2, j]
        )

    def gather_pass(p):
        par = p % 2
        lanes = slice(p * COLS, (p + 1) * COLS)
        own_cols = x_cols(me, p)
        state[par, 0] = jnp.zeros((STATE, COLS), F32)

        @pl.loop(0, N_INNER)
        def _(j):
            slot = xbuf.at[p, rows_of(j)]
            pltpu.make_async_copy(slot, slot, xrecv.at[p, j]).wait()
            weight, bias = wx_ref[:, own_cols], bx_ref[:, own_cols]
            parts = []
            for r in range(0, SPAN, SUB):
                at = pl.ds(pl.multiple_of(j * SPAN + r, SUB), SUB)
                x_r = conv_silu(
                    xbuf[p, pl.ds(pl.multiple_of(j * SPAN + r, EDGE), SUB + EDGE), :], weight, bias
                )
                xc[par, at, :] = x_r
                scaled = (x_r.astype(F32) * dot(coef[at, :], ew[:, lanes])).astype(BF16)
                xs[par, at, :] = scaled
                parts.append(scaled)
            at = pl.ds(pl.multiple_of(j * SPAN, SPAN), SPAN)
            added = dot(bt[at, :], jnp.concatenate(parts, axis=0))
            state[par, j + 1] = dec[j, :, lanes] * (state[par, j] + added)

        ebuf[p] = state[par, N_INNER].astype(BF16)
        for k in range(1, N_SLAB):

            @pl.when(slab + k < N_SLAB)
            def _():
                end_copy(p, k).start()

    def output_pass(p):
        par = p % 2
        lanes = slice(p * COLS, (p + 1) * COLS)
        inc[...] = jnp.zeros((STATE, COLS), F32)

        @pl.loop(0, slab)
        def _(m):
            slot = arr.at[p, m]
            pltpu.make_async_copy(slot, slot, erecv.at[p, m]).wait()
            inc[...] = tot[m, :, lanes] * inc[...] + arr[p, m].astype(F32)

        @pl.loop(0, N_INNER)
        def _(j):
            at = pl.ds(pl.multiple_of(j * SPAN, SPAN), SPAN)
            before = (state[par, j] + ep[j, :, lanes] * inc[...]).astype(BF16)
            acc = dot(gm[at, :], xs[par, at, :]) + dot(cc[at, :], before)
            acc = acc * dot(coef[at, :], ee[:, lanes])
            y = acc + skip[:, lanes] * xc[par, at, :].astype(F32)
            xc[par, at, :] = y.astype(BF16)
            out_copy(p, j).start()

    def out_wait(p):
        @pl.loop(0, N_INNER)
        def _(j):
            out_copy(p, j).wait()

    for p in range(PIECES + 1):
        if p < PIECES:
            if p >= 2:
                out_wait(p - 2)
            gather_pass(p)
        if p >= 1:
            output_pass(p - 1)
    out_wait(PIECES - 2)
    out_wait(PIECES - 1)

    for n in range(N_PEER):
        bc_copy(n, 0).wait_send()
        bc_copy(n, 1).wait_send()
        dt_copy(n).wait_send()
        for p in range(PIECES):
            x_copy(n, p).wait_send()

    @pl.when(halo_out)
    def _():
        @pl.loop(0, N_INNER)
        def _(d):
            for copy in halo_copies(d):
                copy.wait_send()

    for k in range(1, N_SLAB):

        @pl.when(slab + k < N_SLAB)
        def _():
            tot_copy(k).wait_send()
            for p in range(PIECES):
                end_copy(p, k).wait_send()


def shards(
    x_in, bc_in, dt_raw, dt_bias, a_log, d_skip, conv_x_weight, conv_x_bias, conv_bc_weight, conv_bc_bias
):
    tok_slab = N_INNER * SPAN
    whole = pl.BlockSpec(memory_space=pltpu.VMEM)
    anywhere = pl.BlockSpec(memory_space=pl.ANY)
    dma = pltpu.SemaphoreType.DMA
    return pl.pallas_call(
        body,
        out_shape=jax.ShapeDtypeStruct((tok_slab, CH), BF16),
        in_specs=[anywhere, anywhere] + [whole] * 6,
        out_specs=anywhere,
        scratch_shapes=[
            pltpu.VMEM((PIECES, EDGE + tok_slab, COLS), BF16),
            pltpu.VMEM((EDGE + tok_slab, STATE), BF16),
            pltpu.VMEM((EDGE + tok_slab, STATE), BF16),
            pltpu.VMEM((N_INNER, NH, SPAN), BF16),
            pltpu.VMEM((HEADS, SPAN), BF16),
            pltpu.VMEM((tok_slab, SPAN), BF16),
            pltpu.VMEM((tok_slab, STATE), BF16),
            pltpu.VMEM((tok_slab, SPAN), BF16),
            pltpu.VMEM((tok_slab, 128), BF16),
            pltpu.VMEM((128, CH), BF16),
            pltpu.VMEM((128, CH), BF16),
            pltpu.VMEM((N_INNER, 1, CH), F32),
            pltpu.VMEM((N_INNER + 1, 1, CH), F32),
            pltpu.VMEM((N_SLAB, 1, CH), F32),
            pltpu.VMEM((1, CH), F32),
            pltpu.VMEM((2, N_INNER + 1, STATE, COLS), F32),
            pltpu.VMEM((2, tok_slab, COLS), BF16),
            pltpu.VMEM((2, tok_slab, COLS), BF16),
            pltpu.VMEM((PIECES, STATE, COLS), BF16),
            pltpu.VMEM((PIECES, N_SLAB, STATE, COLS), BF16),
            pltpu.VMEM((STATE, COLS), F32),
            dma((PIECES, N_PEER)),
            dma((PIECES, N_INNER)),
            dma((3, N_PEER)),
            dma((3, N_INNER)),
            dma((2 + PIECES, N_INNER)),
            dma((2 + PIECES,)),
            dma((N_SLAB,)),
            dma((N_SLAB,)),
            dma((PIECES, N_SLAB)),
            dma((PIECES, N_SLAB)),
            dma((2, N_INNER)),
        ],
        compiler_params=pltpu.CompilerParams(
            collective_id=0, has_side_effects=True, vmem_limit_bytes=56 * 2**20
        ),
        cost_estimate=pl.CostEstimate(
            flops=9 * 10**9, bytes_accessed=18 * 2**20, transcendentals=6 * 2**20
        ),
    )(
        x_in,
        bc_in,
        dt_raw,
        jnp.stack([dt_bias, a_log, d_skip], axis=1),
        conv_x_weight,
        conv_x_bias[None, :],
        conv_bc_weight,
        conv_bc_bias[None, :],
    )


def solution(mesh):
    rows = P(("slab", "inner"), None)
    return jax.shard_map(
        shards,
        mesh=mesh,
        in_specs=(rows, rows, rows) + (P(),) * 7,
        out_specs=P("slab", "inner"),
        check_vma=False,
    )
```

time: 638 us -> 193 us (0.30)
  the two profiles are of different devices: /device:TPU:1 before, /device:TPU:21 now
where the time goes in v1:
time: 193 us; the launch traced here: 192 us
  Pallas kernels  183 us (95%)
  local copies, waits for them, and re-layouts  8.56 us (4%)
    pallas_call x1, Pallas kernels, shards(): pl.pallas_call(body, out_shape=jax.ShapeDtypeStruct((tok_slab, CH), BF16)...  183 us
    unnamed x1, local copies, waits for them, and re-layouts  7.76 us

profile of v1, /device:TPU:21, one launch (start us, length us, event | category | flops | bytes accessed | tf_op | source)
XLA Modules:
  0.0 192.4 jit_solution(8833920781506836590)
XLA Ops:
  0.0 0.7 pad_maximum_fusion
  0.7 0.8 copy.14.head_ref
  1.5 183.1 %shard_map.100 = bf16[4096,1024]{1,0:T(8,128)(2,1)} custom-call(bf16[256,16384]{1,0:T(8,128)(2,1)} %x_ref.1, bf16[256,4096]{1,0:T(8,128)(2,1)} %bc_ref.1, bf16[256,256]{1,0:T(8,128)(2,1)} %dt_ref.1, f32[256,3]{1,0:T(8,128)} %copy.14.head_ref, f32[4,16384]{1,0:T(4,128)} %wx_ref.1, f32[1,16384]{1,0:T(1,128)} %bitcast.8, f32[4,4096]{1,0:T(4,128)} %wbc_ref.1, ...), custom_call_target="tpu_custom_call" | custom-call | flops 8999999488 | bytes 18874368 | tf_op jit(solution)/shard_map/pallas_call | solution.py:360
  184.6 7.8 %copy.16 = bf16[4096,1024]{1,0:T(8,128)(2,1)} copy(bf16[4096,1024]{1,0:T(8,128)(2,1)} %shard_map.100) | data formatting | bytes 16777216

commit v2 on v1

v2 whole, which is shorter than its diff:
```python
import jax
import jax.numpy as jnp
from jax import lax
from jax.experimental import pallas as pl
from jax.experimental.pallas import tpu as pltpu
from jax.sharding import PartitionSpec as P

HEADS = 256
HEADDIM = 64
STATE = 256
GROUPS = 8
SPAN = 256
N_SLAB = 8
N_INNER = 16
CH = 1024
NH = 16
CUTS = (0, 256, 512, 768, 896, 1024)
PIECES = len(CUTS) - 1
BC = 2 * GROUPS * STATE
C_EARLY = 8
EDGE = 16
SUB = 64
MESH = pl.DeviceIdType.MESH
ORDER = (
    (2, 2), (1, 0), (0, 3), (3, 1), (2, 1), (0, 1), (3, 0), (1, 3),
    (1, 2), (2, 0), (3, 3), (0, 2), (1, 1), (2, 3), (3, 2),
)
N_PEER = len(ORDER)
F32 = jnp.float32
BF16 = jnp.bfloat16


def dot(a, b):
    return jnp.dot(a, b, preferred_element_type=F32)


def conv_silu(rows, weight, bias):
    full = rows.astype(F32)
    n = rows.shape[0] - EDGE
    acc = bias
    for k in range(4):
        start = EDGE - 3 + k
        acc = acc + weight[k : k + 1, :] * full[start : start + n]
    half = 0.5 * acc
    return (half + half * jnp.tanh(half)).astype(BF16)


def body(
    x_ref, bc_ref, dt_ref, bias_ref, alog_ref, skip_ref, wx_ref, bx_ref, wbc_ref, bbc_ref,
    out_ref,
    xbuf, xhalo, edge, bcraw, bcconv, bbuf, cbuf, dtbuf, dt_t, heads, bt, coef, ew, ee, dec, ep, tot, skip,
    state, carry, xs, ebuf, arr, inc,
    xsend, xrecv, ssend, srecv, hsend, hrecv, bhsend, bhrecv, bsem, tsend, trecv, esend, erecv, osem,
):
    slab = lax.axis_index("slab")
    me = lax.axis_index("inner")
    my_z, my_x = me // 4, lax.rem(me, 4)
    sign = 1 - 2 * lax.rem(slab, 2)

    def at_offset(dx, dz, way):
        return lax.rem(my_z + way * dz + 4, 4) * 4 + lax.rem(my_x + way * dx + 4, 4)

    peers = [at_offset(dx, dz, sign) for dx, dz in ORDER]
    sources = [at_offset(dx, dz, -sign) for dx, dz in ORDER]
    halo_out = jnp.logical_and(me == N_INNER - 1, slab < N_SLAB - 1)
    not_first = jnp.logical_or(me > 0, slab > 0)
    not_last = jnp.logical_or(me < N_INNER - 1, slab < N_SLAB - 1)

    barrier = pltpu.get_barrier_semaphore()
    for peer in peers:
        pl.semaphore_signal(barrier, inc=1, device_id=(slab, peer), device_id_type=MESH)
    for k in range(1, N_SLAB):

        @pl.when(slab >= k)
        def _():
            pl.semaphore_signal(barrier, inc=1, device_id=(slab - k, me), device_id_type=MESH)

    @pl.when(slab > 0)
    def _():
        pl.semaphore_signal(barrier, inc=1, device_id=(slab - 1, N_INNER - 1), device_id_type=MESH)

    own_bc = pltpu.make_async_copy(bc_ref, bcraw.at[pl.ds(EDGE, SPAN)], bsem)
    own_bc.start()
    pl.semaphore_wait(
        barrier, N_PEER + (N_SLAB - 1 - slab) + jnp.where(halo_out, N_INNER, 0)
    )

    def block(j):
        return pl.ds(pl.multiple_of(j * SPAN, SPAN), SPAN)

    def lanes_of(p):
        return slice(CUTS[p], CUTS[p + 1])

    def lane_ds(p):
        return pl.ds(CUTS[p], CUTS[p + 1] - CUTS[p])

    def x_cols(d, p):
        return pl.ds(pl.multiple_of(d * CH + CUTS[p], 128), CUTS[p + 1] - CUTS[p])

    def bc_cols(d, which):
        return pl.ds(pl.multiple_of((d // 2 + which * GROUPS) * STATE, STATE), STATE)

    def head_rows(d):
        return pl.ds(pl.multiple_of(d * NH, NH), NH)

    def remote(src, dst, send_sem, recv_sem, to):
        return pltpu.make_async_remote_copy(
            src, dst, send_sem, recv_sem, device_id=to, device_id_type=MESH
        )

    def landed(ref, sem):
        pltpu.make_async_copy(ref, ref, sem).wait()

    def bc_copy(n, which):
        return remote(
            bcconv.at[:, bc_cols(peers[n], which)], (bbuf, cbuf)[which].at[block(me)],
            ssend.at[which, n], srecv.at[which, me], (slab, peers[n]),
        )

    def dt_copy(n):
        return remote(
            dt_t.at[head_rows(peers[n])], dtbuf.at[me], ssend.at[2, n], srecv.at[2, me], (slab, peers[n])
        )

    def x_copy(n, p):
        return remote(
            x_ref.at[:, x_cols(peers[n], p)], xbuf.at[block(me), lane_ds(p)],
            xsend.at[p, n], xrecv.at[p, me], (slab, peers[n]),
        )

    tail = pl.ds(SPAN - EDGE, EDGE)

    def x_halo_copy(d):
        return remote(
            x_ref.at[tail, pl.ds(pl.multiple_of(d * CH, CH), CH)], xhalo, hsend.at[d], hrecv, (slab + 1, d)
        )

    def bc_halo_copy():
        wrap = me // (N_INNER - 1)
        return remote(
            bc_ref.at[tail], bcraw.at[pl.ds(0, EDGE)], bhsend, bhrecv, (slab + wrap, (me + 1) * (1 - wrap))
        )

    @pl.when(not_last)
    def _():
        bc_halo_copy().start()

    for n in range(N_PEER):
        x_copy(n, 0).start()

    dt_t[...] = dt_ref[...].astype(F32).T.astype(BF16)
    for n in range(N_PEER):
        dt_copy(n).start()

    @pl.when(halo_out)
    def _():
        @pl.loop(0, N_INNER)
        def _(d):
            x_halo_copy(d).start()

    own_dt = pltpu.make_async_copy(dt_t.at[head_rows(me)], dtbuf.at[me], srecv.at[2, me])
    own_dt.start()
    for p in range(PIECES):
        pltpu.make_async_copy(
            x_ref.at[:, x_cols(me, p)], xbuf.at[block(me), lane_ds(p)], xrecv.at[p, me]
        ).start()

    @pl.when(not_first)
    def _():
        landed(bcraw.at[pl.ds(0, EDGE)], bhrecv)

    @pl.when(jnp.logical_not(not_first))
    def _():
        bcraw[pl.ds(0, EDGE), :] = jnp.zeros((EDGE, BC), BF16)

    own_bc.wait()

    @pl.loop(0, BC // STATE)
    def _(g):
        cols = pl.ds(pl.multiple_of(g * STATE, STATE), STATE)
        weight, bias = wbc_ref[:, cols], bbc_ref[:, cols]
        for r in range(0, SPAN, SUB):
            bcconv[pl.ds(r, SUB), cols] = conv_silu(bcraw[pl.ds(r, SUB + EDGE), cols], weight, bias)

    for which in range(2):
        pltpu.make_async_copy(
            bcconv.at[:, bc_cols(me, which)], (bbuf, cbuf)[which].at[block(me)], srecv.at[which, me]
        ).start()
    for n in range(N_PEER):
        bc_copy(n, 0).start()
    for p in range(1, PIECES):
        for n in range(N_PEER):
            x_copy(n, p).start()
    for n in range(C_EARLY):
        bc_copy(n, 1).start()

    chan = lax.broadcasted_iota(jnp.int32, (128, CH), 1) // HEADDIM
    row = lax.broadcasted_iota(jnp.int32, (128, CH), 0)
    ew[...] = jnp.where((row < 2 * NH) & (lax.rem(row, NH) == chan), 1.0, 0.0).astype(BF16)
    ee[...] = jnp.where(
        (row >= 2 * NH) & (row < 4 * NH) & (lax.rem(row, NH) == chan), 1.0, 0.0
    ).astype(BF16)
    heads[...] = jnp.concatenate(
        [bias_ref[...], -jnp.exp(alog_ref[...]), skip_ref[...], jnp.zeros((5, HEADS), F32)], axis=0
    ).T
    own_heads = heads[head_rows(me), :]
    bias_col, rate_col, skip_col = own_heads[:, 0:1], own_heads[:, 1:2], own_heads[:, 2:3]
    pick = lax.broadcasted_iota(jnp.int32, (NH, CH), 0) == (
        lax.broadcasted_iota(jnp.int32, (NH, CH), 1) // HEADDIM
    )
    skip[...] = jnp.sum(jnp.where(pick, skip_col, 0.0), axis=0, keepdims=True)
    ep[0] = jnp.ones((1, CH), F32)
    row_ids = lax.broadcasted_iota(jnp.int32, (SPAN, SPAN), 0)
    col_ids = lax.broadcasted_iota(jnp.int32, (SPAN, SPAN), 1)
    upto = jnp.where(row_ids <= col_ids, 1.0, 0.0).astype(F32)

    @pl.when(slab == 0)
    def _():
        edge[...] = jnp.zeros((EDGE, CH), BF16)

    @pl.when(slab > 0)
    def _():
        landed(xhalo, hrecv)
        edge[...] = xhalo[...]

    @pl.loop(0, N_INNER)
    def _(j):
        landed(dtbuf.at[j], srecv.at[2, j])
        raw = dtbuf[j].astype(F32) + bias_col
        dt = jnp.maximum(raw, 0.0) + jnp.log1p(jnp.exp(-jnp.abs(raw)))
        da = dt * rate_col
        cumul = jnp.dot(da, upto, preferred_element_type=F32, precision=lax.Precision.HIGHEST)
        grow = jnp.exp(-cumul) * dt
        decay = jnp.exp(cumul)
        grow_hi = grow.astype(BF16).astype(F32)
        decay_hi = decay.astype(BF16).astype(F32)
        parts = jnp.concatenate(
            [grow_hi, grow - grow_hi, decay_hi, decay - decay_hi, jnp.zeros((4 * NH, SPAN), F32)],
            axis=0,
        )
        coef_j = parts.T.astype(BF16)
        coef[block(j), :] = coef_j
        dec_j = dot(coef_j[SPAN - EDGE :], ee[...])[EDGE - 1 : EDGE]
        dec[j] = dec_j
        ep[j + 1] = ep[j] * dec_j

    def tot_copy(k):
        return remote(ep.at[N_INNER], tot.at[slab], tsend.at[k], trecv.at[slab], (slab + k, me))

    for k in range(1, N_SLAB):

        @pl.when(slab + k < N_SLAB)
        def _():
            tot_copy(k).start()

    @pl.loop(0, slab)
    def _(m):
        landed(tot.at[m], trecv.at[m])

    @pl.loop(0, N_INNER)
    def _(j):
        landed(bbuf.at[block(j)], srecv.at[0, j])
        bt[block(j), :] = bbuf[block(j), :].astype(F32).T.astype(BF16)

    def end_copy(p, k):
        return remote(
            ebuf.at[:, lane_ds(p)], arr.at[slab, :, lane_ds(p)], esend.at[p, k], erecv.at[p, slab],
            (slab + k, me),
        )

    def gather_pass(p):
        lanes = lanes_of(p)
        own_cols = x_cols(me, p)
        width = CUTS[p + 1] - CUTS[p]
        carry[:, :width] = jnp.zeros((STATE, width), F32)

        @pl.loop(0, N_INNER)
        def _(j):
            landed(xbuf.at[block(j), lane_ds(p)], xrecv.at[p, j])
            weight, bias = wx_ref[:, own_cols], bx_ref[:, own_cols]
            before = edge[:, lanes]
            edge[:, lanes] = xbuf[pl.ds(pl.multiple_of((j + 1) * SPAN - EDGE, EDGE), EDGE), lanes]
            parts = []
            for r in reversed(range(0, SPAN, SUB)):
                at = pl.ds(pl.multiple_of(j * SPAN + r, SUB), SUB)
                if r:
                    rows = xbuf[pl.ds(pl.multiple_of(j * SPAN + r - EDGE, EDGE), SUB + EDGE), lanes]
                else:
                    rows = jnp.concatenate([before, xbuf[at, lanes]], axis=0)
                x_r = conv_silu(rows, weight, bias)
                xbuf[at, lanes] = x_r
                scaled = (x_r.astype(F32) * dot(coef[at, :], ew[:, lanes])).astype(BF16)
                xs[at, lanes] = scaled
                parts.insert(0, scaled)
            added = dot(bt[block(j), :], jnp.concatenate(parts, axis=0))
            now = carry[:, :width]
            state[j, :, lanes] = now
            carry[:, :width] = dec[j, :, lanes] * (now + added)

        ebuf[:, lanes] = carry[:, :width].astype(BF16)
        for k in range(1, N_SLAB):

            @pl.when(slab + k < N_SLAB)
            def _():
                end_copy(p, k).start()

    def incoming_pass(p):
        lanes = lanes_of(p)
        inc[:, lanes] = jnp.zeros((STATE, CUTS[p + 1] - CUTS[p]), F32)

        @pl.loop(0, slab)
        def _(m):
            landed(arr.at[m, :, lane_ds(p)], erecv.at[p, m])
            inc[:, lanes] = tot[m, :, lanes] * inc[:, lanes] + arr[m, :, lanes].astype(F32)

    for p in range(PIECES):
        gather_pass(p)
        if p == PIECES - 1:
            for n in range(C_EARLY, N_PEER):
                bc_copy(n, 1).start()
        if p:
            incoming_pass(p - 1)
    incoming_pass(PIECES - 1)

    def out_copy(j):
        return pltpu.make_async_copy(xs.at[block(j)], out_ref.at[block(j)], osem.at[j])

    @pl.loop(0, N_INNER)
    def _(i):
        j = me
        for n in range(N_PEER):
            j = jnp.where(i == n + 1, sources[n], j)
        landed(cbuf.at[block(j)], srecv.at[1, j])
        c_j = cbuf[block(j), :]
        g_j = jnp.where(row_ids >= col_ids, dot(c_j, bt[block(j), :]), 0.0).astype(BF16)
        for q in range(0, CH, 256):
            lanes = slice(q, q + 256)
            before = (state[j, :, lanes] + ep[j, :, lanes] * inc[:, lanes]).astype(BF16)
            acc = dot(g_j, xs[block(j), lanes]) + dot(c_j, before)
            acc = acc * dot(coef[block(j), :], ee[:, lanes])
            y = acc + skip[:, lanes] * xbuf[block(j), lanes].astype(F32)
            xs[block(j), lanes] = y.astype(BF16)
        out_copy(j).start()

    @pl.loop(0, N_INNER)
    def _(j):
        out_copy(j).wait()

    for n in range(N_PEER):
        bc_copy(n, 0).wait_send()
        bc_copy(n, 1).wait_send()
        dt_copy(n).wait_send()
        for p in range(PIECES):
            x_copy(n, p).wait_send()

    @pl.when(halo_out)
    def _():
        @pl.loop(0, N_INNER)
        def _(d):
            x_halo_copy(d).wait_send()

    @pl.when(not_last)
    def _():
        bc_halo_copy().wait_send()

    for k in range(1, N_SLAB):

        @pl.when(slab + k < N_SLAB)
        def _():
            tot_copy(k).wait_send()
            for p in range(PIECES):
                end_copy(p, k).wait_send()


def hand_over(y_ref, out_ref, sem):
    def copy(j):
        at = pl.ds(pl.multiple_of(j * SPAN, SPAN), SPAN)
        return pltpu.make_async_copy(y_ref.at[at], out_ref.at[at], sem.at[j])

    @pl.loop(0, N_INNER)
    def _(j):
        copy(j).start()

    @pl.loop(0, N_INNER)
    def _(j):
        copy(j).wait()


def shards(
    x_in, bc_in, dt_raw, dt_bias, a_log, d_skip, conv_x_weight, conv_x_bias, conv_bc_weight, conv_bc_bias
):
    tok_slab = N_INNER * SPAN
    whole = pl.BlockSpec(memory_space=pltpu.VMEM)
    anywhere = pl.BlockSpec(memory_space=pl.ANY)
    dma = pltpu.SemaphoreType.DMA
    y = pl.pallas_call(
        body,
        out_shape=jax.ShapeDtypeStruct((tok_slab, CH), BF16),
        in_specs=[anywhere, anywhere] + [whole] * 8,
        out_specs=anywhere,
        scratch_shapes=[
            pltpu.VMEM((tok_slab, CH), BF16),
            pltpu.VMEM((EDGE, CH), BF16),
            pltpu.VMEM((EDGE, CH), BF16),
            pltpu.VMEM((EDGE + SPAN, BC), BF16),
            pltpu.VMEM((SPAN, BC), BF16),
            pltpu.VMEM((tok_slab, STATE), BF16),
            pltpu.VMEM((tok_slab, STATE), BF16),
            pltpu.VMEM((N_INNER, NH, SPAN), BF16),
            pltpu.VMEM((HEADS, SPAN), BF16),
            pltpu.VMEM((HEADS, 8), F32),
            pltpu.VMEM((tok_slab, SPAN), BF16),
            pltpu.VMEM((tok_slab, 128), BF16),
            pltpu.VMEM((128, CH), BF16),
            pltpu.VMEM((128, CH), BF16),
            pltpu.VMEM((N_INNER, 1, CH), F32),
            pltpu.VMEM((N_INNER + 1, 1, CH), F32),
            pltpu.VMEM((N_SLAB, 1, CH), F32),
            pltpu.VMEM((1, CH), F32),
            pltpu.VMEM((N_INNER, STATE, CH), F32),
            pltpu.VMEM((STATE, 256), F32),
            pltpu.VMEM((tok_slab, CH), BF16),
            pltpu.VMEM((STATE, CH), BF16),
            pltpu.VMEM((N_SLAB, STATE, CH), BF16),
            pltpu.VMEM((STATE, CH), F32),
            dma((PIECES, N_PEER)),
            dma((PIECES, N_INNER)),
            dma((3, N_PEER)),
            dma((3, N_INNER)),
            dma((N_INNER,)),
            dma,
            dma,
            dma,
            dma,
            dma((N_SLAB,)),
            dma((N_SLAB,)),
            dma((PIECES, N_SLAB)),
            dma((PIECES, N_SLAB)),
            dma((N_INNER,)),
        ],
        compiler_params=pltpu.CompilerParams(
            collective_id=0, has_side_effects=True, vmem_limit_bytes=58 * 2**20
        ),
        cost_estimate=pl.CostEstimate(
            flops=9 * 10**9, bytes_accessed=18 * 2**20, transcendentals=6 * 2**20
        ),
    )(
        x_in,
        bc_in,
        dt_raw,
        dt_bias[None, :],
        a_log[None, :],
        d_skip[None, :],
        conv_x_weight,
        conv_x_bias[None, :],
        conv_bc_weight,
        conv_bc_bias[None, :],
    )
    return pl.pallas_call(
        hand_over,
        out_shape=jax.ShapeDtypeStruct((tok_slab, CH), BF16),
        in_specs=[anywhere],
        out_specs=anywhere,
        scratch_shapes=[dma((N_INNER,))],
        compiler_params=pltpu.CompilerParams(vmem_limit_bytes=56 * 2**20),
        cost_estimate=pl.CostEstimate(flops=0, bytes_accessed=16 * 2**20, transcendentals=0),
    )(y)


def solution(mesh):
    rows = P(("slab", "inner"), None)
    return jax.shard_map(
        shards,
        mesh=mesh,
        in_specs=(rows, rows, rows) + (P(),) * 7,
        out_specs=P("slab", "inner"),
        check_vma=False,
    )
```

time: 193 us -> 420 us (2.18)
  the two profiles are of different devices: /device:TPU:21 before, /device:TPU:24 now
where the time goes in v2:
time: 420 us; the launch traced here: 418 us
  Pallas kernels  418 us (100%)
    pallas_call x1, Pallas kernels, shards(): pl.pallas_call(hand_over, out_shape=jax.ShapeDtypeStruct((tok_slab, CH),...  255 us
    pallas_call x1, Pallas kernels, shards(): pl.pallas_call(body, out_shape=jax.ShapeDtypeStruct((tok_slab, CH), BF16)...  163 us

profile of v2, /device:TPU:24, one launch (start us, length us, event | category | flops | bytes accessed | tf_op | source)
XLA Modules:
  0.0 418.1 jit_solution(16275741853346518114)
XLA Ops:
  0.0 162.8 %shard_map.100.y_ref = bf16[4096,1024]{1,0:T(8,128)(2,1)} custom-call(bf16[256,16384]{1,0:T(8,128)(2,1)} %x_ref.1, bf16[256,4096]{1,0:T(8,128)(2,1)} %bc_ref.1, bf16[256,256]{1,0:T(8,128)(2,1)} %dt_ref.1, f32[1,256]{1,0:T(1,128)} %bitcast.7, f32[1,256]{1,0:T(1,128)} %bitcast.8, f32[1,256]{1,0:T(1,128)} %bitcast.9, f32[4,16384]{1,0:T(4,128)} %wx_ref.1, ...), custom_call_target="tpu_custom_call" | custom-call | flops 8999999488 | bytes 18874368 | tf_op jit(solution)/shard_map/pallas_call | solution.py:396
  162.8 255.4 %shard_map.101 = bf16[4096,1024]{1,0:T(8,128)(2,1)} custom-call(bf16[4096,1024]{1,0:T(8,128)(2,1)} %shard_map.100.y_ref), custom_call_target="tpu_custom_call" | custom-call | bytes 16777216 | tf_op jit(solution)/shard_map/pallas_call | solution.py:459

commit v3 on v2

--- a/solution.py
+++ b/solution.py
@@ -372,18 +372,28 @@
                 end_copy(p, k).wait_send()
 
 
-def hand_over(y_ref, out_ref, sem):
-    def copy(j):
-        at = pl.ds(pl.multiple_of(j * SPAN, SPAN), SPAN)
-        return pltpu.make_async_copy(y_ref.at[at], out_ref.at[at], sem.at[j])
-
-    @pl.loop(0, N_INNER)
-    def _(j):
-        copy(j).start()
-
-    @pl.loop(0, N_INNER)
-    def _(j):
-        copy(j).wait()
+def hand_over(y_ref, out_ref, buf, isem, osem):
+    def at(j):
+        return pl.ds(pl.multiple_of(j * SPAN, SPAN), SPAN)
+
+    def read(j):
+        return pltpu.make_async_copy(y_ref.at[at(j)], buf.at[at(j)], isem.at[j])
+
+    def write(j):
+        return pltpu.make_async_copy(buf.at[at(j)], out_ref.at[at(j)], osem.at[j])
+
+    @pl.loop(0, N_INNER)
+    def _(j):
+        read(j).start()
+
+    @pl.loop(0, N_INNER)
+    def _(j):
+        read(j).wait()
+        write(j).start()
+
+    @pl.loop(0, N_INNER)
+    def _(j):
+        write(j).wait()
 
 
 def shards(
@@ -461,7 +471,7 @@
         out_shape=jax.ShapeDtypeStruct((tok_slab, CH), BF16),
         in_specs=[anywhere],
         out_specs=anywhere,
-        scratch_shapes=[dma((N_INNER,))],
+        scratch_shapes=[pltpu.VMEM((tok_slab, CH), BF16), dma((N_INNER,)), dma((N_INNER,))],
         compiler_params=pltpu.CompilerParams(vmem_limit_bytes=56 * 2**20),
         cost_estimate=pl.CostEstimate(flops=0, bytes_accessed=16 * 2**20, transcendentals=0),
     )(y)

time: 420 us -> 171 us (0.41)
  Pallas kernels: 418 us -> 169 us
    pallas_call x1, Pallas kernels: 255 us -> 6.55 us  [shards(): pl.pallas_call(hand_over, out_shape=jax.ShapeDtypeStruct((tok_slab, CH),...]
where the time goes in v3:
time: 171 us; the launch traced here: 169 us
  Pallas kernels  169 us (99%)
    pallas_call x1, Pallas kernels, shards(): pl.pallas_call(body, out_shape=jax.ShapeDtypeStruct((tok_slab, CH), BF16)...  163 us
    pallas_call x1, Pallas kernels, shards(): pl.pallas_call(hand_over, out_shape=jax.ShapeDtypeStruct((tok_slab, CH),...  6.55 us

profile of v3, /device:TPU:24, one launch (start us, length us, event | category | flops | bytes accessed | tf_op | source)
XLA Modules:
  0.0 169.3 jit_solution(3960214844130668447)
XLA Ops:
  0.0 162.8 %shard_map.100.y_ref = bf16[4096,1024]{1,0:T(8,128)(2,1)} custom-call(bf16[256,16384]{1,0:T(8,128)(2,1)} %x_ref.1, bf16[256,4096]{1,0:T(8,128)(2,1)} %bc_ref.1, bf16[256,256]{1,0:T(8,128)(2,1)} %dt_ref.1, f32[1,256]{1,0:T(1,128)} %bitcast.7, f32[1,256]{1,0:T(1,128)} %bitcast.8, f32[1,256]{1,0:T(1,128)} %bitcast.9, f32[4,16384]{1,0:T(4,128)} %wx_ref.1, ...), custom_call_target="tpu_custom_call" | custom-call | flops 8999999488 | bytes 18874368 | tf_op jit(solution)/shard_map/pallas_call | solution.py:406
  162.8 6.5 %shard_map.101 = bf16[4096,1024]{1,0:T(8,128)(2,1)} custom-call(bf16[4096,1024]{1,0:T(8,128)(2,1)} %shard_map.100.y_ref), custom_call_target="tpu_custom_call" | custom-call | bytes 16777216 | tf_op jit(solution)/shard_map/pallas_call | solution.py:469

commit v4 on v3

--- a/solution.py
+++ b/solution.py
@@ -17,7 +17,7 @@
 CUTS = (0, 256, 512, 768, 896, 1024)
 PIECES = len(CUTS) - 1
 BC = 2 * GROUPS * STATE
-C_EARLY = 8
+C_EARLY = 11
 EDGE = 16
 SUB = 64
 MESH = pl.DeviceIdType.MESH
@@ -48,9 +48,9 @@
 def body(
     x_ref, bc_ref, dt_ref, bias_ref, alog_ref, skip_ref, wx_ref, bx_ref, wbc_ref, bbc_ref,
     out_ref,
-    xbuf, xhalo, edge, bcraw, bcconv, bbuf, cbuf, dtbuf, dt_t, heads, bt, coef, ew, ee, dec, ep, tot, skip,
+    xbuf, xlast, xpack, xhalo, edge, bcraw, bctail, bchalo, bcconv, bbuf, cbuf, dtbuf, dt_t, heads, bt, coef, ew, ee, dec, ep, tot, skip,
     state, carry, xs, ebuf, arr, inc,
-    xsend, xrecv, ssend, srecv, hsend, hrecv, bhsend, bhrecv, bsem, tsend, trecv, esend, erecv, osem,
+    xsend, xrecv, ssend, srecv, hsend, hrecv, bhsend, bhrecv, bsem, lsem, tsend, trecv, esend, erecv, osem,
 ):
     slab = lax.axis_index("slab")
     me = lax.axis_index("inner")
@@ -62,7 +62,6 @@
 
     peers = [at_offset(dx, dz, sign) for dx, dz in ORDER]
     sources = [at_offset(dx, dz, -sign) for dx, dz in ORDER]
-    halo_out = jnp.logical_and(me == N_INNER - 1, slab < N_SLAB - 1)
     not_first = jnp.logical_or(me > 0, slab > 0)
     not_last = jnp.logical_or(me < N_INNER - 1, slab < N_SLAB - 1)
 
@@ -81,6 +80,13 @@
 
     own_bc = pltpu.make_async_copy(bc_ref, bcraw.at[pl.ds(EDGE, SPAN)], bsem)
     own_bc.start()
+    halo_out = jnp.logical_and(me == N_INNER - 1, slab < N_SLAB - 1)
+    own_last = pltpu.make_async_copy(x_ref.at[pl.ds(SPAN - EDGE, EDGE)], xlast, lsem)
+
+    @pl.when(halo_out)
+    def _():
+        own_last.start()
+
     pl.semaphore_wait(
         barrier, N_PEER + (N_SLAB - 1 - slab) + jnp.where(halo_out, N_INNER, 0)
     )
@@ -128,18 +134,29 @@
             xsend.at[p, n], xrecv.at[p, me], (slab, peers[n]),
         )
 
-    tail = pl.ds(SPAN - EDGE, EDGE)
-
     def x_halo_copy(d):
-        return remote(
-            x_ref.at[tail, pl.ds(pl.multiple_of(d * CH, CH), CH)], xhalo, hsend.at[d], hrecv, (slab + 1, d)
-        )
+        return remote(xpack.at[d], xhalo, hsend.at[d], hrecv, (slab + 1, d))
 
     def bc_halo_copy():
         wrap = me // (N_INNER - 1)
-        return remote(
-            bc_ref.at[tail], bcraw.at[pl.ds(0, EDGE)], bhsend, bhrecv, (slab + wrap, (me + 1) * (1 - wrap))
-        )
+        return remote(bctail, bchalo, bhsend, bhrecv, (slab + wrap, (me + 1) * (1 - wrap)))
+
+    def pack(rows, width):
+        last = rows.astype(F32)[EDGE - 3 :]
+        groups = rows.shape[1] // width
+        return jnp.concatenate(
+            [last[:, q * width : (q + 1) * width] for q in range(groups)]
+            + [jnp.zeros((EDGE - 3 * groups, width), F32)],
+            axis=0,
+        ).astype(BF16)
+
+    def unpack(packed, q):
+        return jnp.concatenate(
+            [jnp.zeros((EDGE - 3, packed.shape[1]), F32), packed.astype(F32)[3 * q : 3 * q + 3]], axis=0
+        ).astype(BF16)
+
+    own_bc.wait()
+    bctail[...] = pack(bcraw[pl.ds(SPAN, EDGE), :], CH)
 
     @pl.when(not_last)
     def _():
@@ -147,16 +164,19 @@
 
     for n in range(N_PEER):
         x_copy(n, 0).start()
+
+    @pl.when(halo_out)
+    def _():
+        own_last.wait()
+
+        @pl.loop(0, N_INNER)
+        def _(d):
+            xpack[d] = pack(xlast[:, pl.ds(pl.multiple_of(d * CH, CH), CH)], 256)
+            x_halo_copy(d).start()
 
     dt_t[...] = dt_ref[...].astype(F32).T.astype(BF16)
     for n in range(N_PEER):
         dt_copy(n).start()
-
-    @pl.when(halo_out)
-    def _():
-        @pl.loop(0, N_INNER)
-        def _(d):
-            x_halo_copy(d).start()
 
     own_dt = pltpu.make_async_copy(dt_t.at[head_rows(me)], dtbuf.at[me], srecv.at[2, me])
     own_dt.start()
@@ -167,13 +187,13 @@
 
     @pl.when(not_first)
     def _():
-        landed(bcraw.at[pl.ds(0, EDGE)], bhrecv)
+        landed(bchalo, bhrecv)
+        for q in range(BC // CH):
+            bcraw[pl.ds(0, EDGE), q * CH : (q + 1) * CH] = unpack(bchalo[...], q)
 
     @pl.when(jnp.logical_not(not_first))
     def _():
         bcraw[pl.ds(0, EDGE), :] = jnp.zeros((EDGE, BC), BF16)
-
-    own_bc.wait()
 
     @pl.loop(0, BC // STATE)
     def _(g):
@@ -188,11 +208,8 @@
         ).start()
     for n in range(N_PEER):
         bc_copy(n, 0).start()
-    for p in range(1, PIECES):
-        for n in range(N_PEER):
-            x_copy(n, p).start()
-    for n in range(C_EARLY):
-        bc_copy(n, 1).start()
+    for n in range(N_PEER):
+        x_copy(n, 1).start()
 
     chan = lax.broadcasted_iota(jnp.int32, (128, CH), 1) // HEADDIM
     row = lax.broadcasted_iota(jnp.int32, (128, CH), 0)
@@ -214,15 +231,6 @@
     col_ids = lax.broadcasted_iota(jnp.int32, (SPAN, SPAN), 1)
     upto = jnp.where(row_ids <= col_ids, 1.0, 0.0).astype(F32)
 
-    @pl.when(slab == 0)
-    def _():
-        edge[...] = jnp.zeros((EDGE, CH), BF16)
-
-    @pl.when(slab > 0)
-    def _():
-        landed(xhalo, hrecv)
-        edge[...] = xhalo[...]
-
     @pl.loop(0, N_INNER)
     def _(j):
         landed(dtbuf.at[j], srecv.at[2, j])
@@ -273,6 +281,18 @@
         own_cols = x_cols(me, p)
         width = CUTS[p + 1] - CUTS[p]
         carry[:, :width] = jnp.zeros((STATE, width), F32)
+
+        if p == 0:
+
+            @pl.when(slab > 0)
+            def _():
+                landed(xhalo, hrecv)
+                for q in range(CH // 256):
+                    edge[:, q * 256 : (q + 1) * 256] = unpack(xhalo[...], q)
+
+            @pl.when(slab == 0)
+            def _():
+                edge[...] = jnp.zeros((EDGE, CH), BF16)
 
         @pl.loop(0, N_INNER)
         def _(j):
@@ -315,6 +335,12 @@
 
     for p in range(PIECES):
         gather_pass(p)
+        if p + 2 < PIECES:
+            for n in range(N_PEER):
+                x_copy(n, p + 2).start()
+        if p == PIECES - 2:
+            for n in range(C_EARLY):
+                bc_copy(n, 1).start()
         if p == PIECES - 1:
             for n in range(C_EARLY, N_PEER):
                 bc_copy(n, 1).start()
@@ -410,9 +436,13 @@
         out_specs=anywhere,
         scratch_shapes=[
             pltpu.VMEM((tok_slab, CH), BF16),
+            pltpu.VMEM((EDGE, N_INNER * CH), BF16),
+            pltpu.VMEM((N_INNER, EDGE, 256), BF16),
+            pltpu.VMEM((EDGE, 256), BF16),
+            pltpu.VMEM((EDGE, CH), BF16),
+            pltpu.VMEM((EDGE + SPAN, BC), BF16),
             pltpu.VMEM((EDGE, CH), BF16),
             pltpu.VMEM((EDGE, CH), BF16),
-            pltpu.VMEM((EDGE + SPAN, BC), BF16),
             pltpu.VMEM((SPAN, BC), BF16),
             pltpu.VMEM((tok_slab, STATE), BF16),
             pltpu.VMEM((tok_slab, STATE), BF16),
@@ -438,6 +468,7 @@
             dma((3, N_PEER)),
             dma((3, N_INNER)),
             dma((N_INNER,)),
+            dma,
             dma,
             dma,
             dma,

time: 171 us -> 167 us (0.977); the launches traced: 169 us -> 167 us
  Pallas kernels: 169 us -> 167 us
    pallas_call x1, Pallas kernels: 163 us -> 161 us  [shards(): pl.pallas_call(body, out_shape=jax.ShapeDtypeStruct((tok_slab, CH), BF16)...]
where the time goes in v4:
time: 167 us
  Pallas kernels  167 us (100%)
    pallas_call x1, Pallas kernels, shards(): pl.pallas_call(body, out_shape=jax.ShapeDtypeStruct((tok_slab, CH), BF16)...  161 us
    pallas_call x1, Pallas kernels, shards(): pl.pallas_call(hand_over, out_shape=jax.ShapeDtypeStruct((tok_slab, CH),...  6.55 us

profile of v4, /device:TPU:24, one launch (start us, length us, event | category | flops | bytes accessed | tf_op | source)
XLA Modules:
  0.0 167.3 jit_solution(3499001175387077032)
XLA Ops:
  0.0 160.7 %shard_map.100.y_ref = bf16[4096,1024]{1,0:T(8,128)(2,1)} custom-call(bf16[256,16384]{1,0:T(8,128)(2,1)} %x_ref.1, bf16[256,4096]{1,0:T(8,128)(2,1)} %bc_ref.1, bf16[256,256]{1,0:T(8,128)(2,1)} %dt_ref.1, f32[1,256]{1,0:T(1,128)} %bitcast.7, f32[1,256]{1,0:T(1,128)} %bitcast.8, f32[1,256]{1,0:T(1,128)} %bitcast.9, f32[4,16384]{1,0:T(4,128)} %wx_ref.1, ...), custom_call_target="tpu_custom_call" | custom-call | flops 8999999488 | bytes 18874368 | tf_op jit(solution)/shard_map/pallas_call | solution.py:432
  160.8 6.5 %shard_map.101 = bf16[4096,1024]{1,0:T(8,128)(2,1)} custom-call(bf16[4096,1024]{1,0:T(8,128)(2,1)} %shard_map.100.y_ref), custom_call_target="tpu_custom_call" | custom-call | bytes 16777216 | tf_op jit(solution)/shard_map/pallas_call | solution.py:500

commit v5 on v4

--- a/solution.py
+++ b/solution.py
@@ -17,8 +17,10 @@
 CUTS = (0, 256, 512, 768, 896, 1024)
 PIECES = len(CUTS) - 1
 BC = 2 * GROUPS * STATE
-C_EARLY = 11
+C_EARLY = 8
 EDGE = 16
+PART = 512
+N_PART = 8
 SUB = 64
 MESH = pl.DeviceIdType.MESH
 ORDER = (
@@ -46,8 +48,9 @@
 
 
 def body(
-    x_ref, bc_ref, dt_ref, bias_ref, alog_ref, skip_ref, wx_ref, bx_ref, wbc_ref, bbc_ref,
+    x_ref, bc_ref, dt_in, bias_in, alog_in, skip_in, wx_in, bx_in, wbc_in, bbc_in,
     out_ref,
+    dt_ref, bias_ref, alog_ref, skip_ref, wx_ref, bx_ref, wbc_ref, bbc_ref, psem,
     xbuf, xlast, xpack, xhalo, edge, bcraw, bctail, bchalo, bcconv, bbuf, cbuf, dtbuf, dt_t, heads, bt, coef, ew, ee, dec, ep, tot, skip,
     state, carry, xs, ebuf, arr, inc,
     xsend, xrecv, ssend, srecv, hsend, hrecv, bhsend, bhrecv, bsem, lsem, tsend, trecv, esend, erecv, osem,
@@ -78,8 +81,25 @@
     def _():
         pl.semaphore_signal(barrier, inc=1, device_id=(slab - 1, N_INNER - 1), device_id_type=MESH)
 
+    small = [
+        pltpu.make_async_copy(src, dst, psem.at[k])
+        for k, (src, dst) in enumerate(
+            [
+                (dt_in, dt_ref),
+                (wbc_in, wbc_ref),
+                (bbc_in, bbc_ref),
+                (bias_in, bias_ref),
+                (alog_in, alog_ref),
+                (skip_in, skip_ref),
+                (wx_in, wx_ref),
+                (bx_in, bx_ref),
+            ]
+        )
+    ]
     own_bc = pltpu.make_async_copy(bc_ref, bcraw.at[pl.ds(EDGE, SPAN)], bsem)
     own_bc.start()
+    for copy in small:
+        copy.start()
     halo_out = jnp.logical_and(me == N_INNER - 1, slab < N_SLAB - 1)
     own_last = pltpu.make_async_copy(x_ref.at[pl.ds(SPAN - EDGE, EDGE)], xlast, lsem)
 
@@ -174,6 +194,8 @@
             xpack[d] = pack(xlast[:, pl.ds(pl.multiple_of(d * CH, CH), CH)], 256)
             x_halo_copy(d).start()
 
+    for copy in small:
+        copy.wait()
     dt_t[...] = dt_ref[...].astype(F32).T.astype(BF16)
     for n in range(N_PEER):
         dt_copy(n).start()
@@ -208,8 +230,9 @@
         ).start()
     for n in range(N_PEER):
         bc_copy(n, 0).start()
-    for n in range(N_PEER):
-        x_copy(n, 1).start()
+    for p in (1, 2):
+        for n in range(N_PEER):
+            x_copy(n, p).start()
 
     chan = lax.broadcasted_iota(jnp.int32, (128, CH), 1) // HEADDIM
     row = lax.broadcasted_iota(jnp.int32, (128, CH), 0)
@@ -335,10 +358,10 @@
 
     for p in range(PIECES):
         gather_pass(p)
-        if p + 2 < PIECES:
+        if p in (0, 1):
             for n in range(N_PEER):
-                x_copy(n, p + 2).start()
-        if p == PIECES - 2:
+                x_copy(n, p + 3).start()
+        if p == PIECES - 3:
             for n in range(C_EARLY):
                 bc_copy(n, 1).start()
         if p == PIECES - 1:
@@ -400,7 +423,7 @@
 
 def hand_over(y_ref, out_ref, buf, isem, osem):
     def at(j):
-        return pl.ds(pl.multiple_of(j * SPAN, SPAN), SPAN)
+        return pl.ds(pl.multiple_of(j * PART, PART), PART)
 
     def read(j):
         return pltpu.make_async_copy(y_ref.at[at(j)], buf.at[at(j)], isem.at[j])
@@ -408,16 +431,16 @@
     def write(j):
         return pltpu.make_async_copy(buf.at[at(j)], out_ref.at[at(j)], osem.at[j])
 
-    @pl.loop(0, N_INNER)
+    @pl.loop(0, N_PART)
     def _(j):
         read(j).start()
 
-    @pl.loop(0, N_INNER)
+    @pl.loop(0, N_PART)
     def _(j):
         read(j).wait()
         write(j).start()
 
-    @pl.loop(0, N_INNER)
+    @pl.loop(0, N_PART)
     def _(j):
         write(j).wait()
 
@@ -426,15 +449,23 @@
     x_in, bc_in, dt_raw, dt_bias, a_log, d_skip, conv_x_weight, conv_x_bias, conv_bc_weight, conv_bc_bias
 ):
     tok_slab = N_INNER * SPAN
-    whole = pl.BlockSpec(memory_space=pltpu.VMEM)
     anywhere = pl.BlockSpec(memory_space=pl.ANY)
     dma = pltpu.SemaphoreType.DMA
     y = pl.pallas_call(
         body,
         out_shape=jax.ShapeDtypeStruct((tok_slab, CH), BF16),
-        in_specs=[anywhere, anywhere] + [whole] * 8,
+        in_specs=[anywhere] * 10,
         out_specs=anywhere,
         scratch_shapes=[
+            pltpu.VMEM((SPAN, HEADS), BF16),
+            pltpu.VMEM((1, HEADS), F32),
+            pltpu.VMEM((1, HEADS), F32),
+            pltpu.VMEM((1, HEADS), F32),
+            pltpu.VMEM((4, N_INNER * CH), F32),
+            pltpu.VMEM((1, N_INNER * CH), F32),
+            pltpu.VMEM((4, BC), F32),
+            pltpu.VMEM((1, BC), F32),
+            dma((8,)),
             pltpu.VMEM((tok_slab, CH), BF16),
             pltpu.VMEM((EDGE, N_INNER * CH), BF16),
             pltpu.VMEM((N_INNER, EDGE, 256), BF16),
@@ -502,7 +533,7 @@
         out_shape=jax.ShapeDtypeStruct((tok_slab, CH), BF16),
         in_specs=[anywhere],
         out_specs=anywhere,
-        scratch_shapes=[pltpu.VMEM((tok_slab, CH), BF16), dma((N_INNER,)), dma((N_INNER,))],
+        scratch_shapes=[pltpu.VMEM((tok_slab, CH), BF16), dma((N_PART,)), dma((N_PART,))],
         compiler_params=pltpu.CompilerParams(vmem_limit_bytes=56 * 2**20),
         cost_estimate=pl.CostEstimate(flops=0, bytes_accessed=16 * 2**20, transcendentals=0),
     )(y)

time: 167 us -> 166 us (level); the launches traced: 167 us -> 164 us
  Pallas kernels: 167 us -> 164 us
    pallas_call x1, Pallas kernels: 161 us -> 158 us  [shards(): pl.pallas_call(body, out_shape=jax.ShapeDtypeStruct((tok_slab, CH), BF16)...]
where the time goes in v5:
time: 166 us; the launch traced here: 164 us
  Pallas kernels  164 us (99%)
    pallas_call x1, Pallas kernels, shards(): pl.pallas_call(body, out_shape=jax.ShapeDtypeStruct((tok_slab, CH), BF16)...  158 us
    pallas_call x1, Pallas kernels, shards(): pl.pallas_call(hand_over, out_shape=jax.ShapeDtypeStruct((tok_slab, CH),...  6.43 us

profile of v5, /device:TPU:24, one launch (start us, length us, event | category | flops | bytes accessed | tf_op | source)
XLA Modules:
  0.0 164.4 jit_solution(12041389049240592617)
XLA Ops:
  0.0 157.9 %shard_map.100.y_ref = bf16[4096,1024]{1,0:T(8,128)(2,1)} custom-call(bf16[256,16384]{1,0:T(8,128)(2,1)} %x_ref.1, bf16[256,4096]{1,0:T(8,128)(2,1)} %bc_ref.1, bf16[256,256]{1,0:T(8,128)(2,1)} %dt_in.1, f32[1,256]{1,0:T(1,128)} %bitcast.7, f32[1,256]{1,0:T(1,128)} %bitcast.8, f32[1,256]{1,0:T(1,128)} %bitcast.9, f32[4,16384]{1,0:T(4,128)} %wx_in.1, ...), custom_call_target="tpu_custom_call" | custom-call | flops 8999999488 | bytes 18874368 | tf_op jit(solution)/shard_map/pallas_call | solution.py:454
  157.9 6.4 %shard_map.101 = bf16[4096,1024]{1,0:T(8,128)(2,1)} custom-call(bf16[4096,1024]{1,0:T(8,128)(2,1)} %shard_map.100.y_ref), custom_call_target="tpu_custom_call" | custom-call | bytes 16777216 | tf_op jit(solution)/shard_map/pallas_call | solution.py:531

commit v6 on v5

--- a/solution.py
+++ b/solution.py
@@ -175,6 +175,9 @@
             [jnp.zeros((EDGE - 3, packed.shape[1]), F32), packed.astype(F32)[3 * q : 3 * q + 3]], axis=0
         ).astype(BF16)
 
+    for n in range(4):
+        x_copy(n, 0).start()
+
     own_bc.wait()
     bctail[...] = pack(bcraw[pl.ds(SPAN, EDGE), :], CH)
 
@@ -182,7 +185,7 @@
     def _():
         bc_halo_copy().start()
 
-    for n in range(N_PEER):
+    for n in range(4, N_PEER):
         x_copy(n, 0).start()
 
     @pl.when(halo_out)

time: 166 us -> 166 us (level)
  no operation moved by 1% of the time
where the time goes in v6:
time: 166 us; the launch traced here: 163 us
  Pallas kernels  163 us (98%)
    pallas_call x1, Pallas kernels, shards(): pl.pallas_call(body, out_shape=jax.ShapeDtypeStruct((tok_slab, CH), BF16)...  157 us
    pallas_call x1, Pallas kernels, shards(): pl.pallas_call(hand_over, out_shape=jax.ShapeDtypeStruct((tok_slab, CH),...  6.43 us

profile of v6, /device:TPU:24, one launch (start us, length us, event | category | flops | bytes accessed | tf_op | source)
XLA Modules:
  0.0 163.2 jit_solution(1153520989287234369)
XLA Ops:
  0.0 156.7 %shard_map.100.y_ref = bf16[4096,1024]{1,0:T(8,128)(2,1)} custom-call(bf16[256,16384]{1,0:T(8,128)(2,1)} %x_ref.1, bf16[256,4096]{1,0:T(8,128)(2,1)} %bc_ref.1, bf16[256,256]{1,0:T(8,128)(2,1)} %dt_in.1, f32[1,256]{1,0:T(1,128)} %bitcast.7, f32[1,256]{1,0:T(1,128)} %bitcast.8, f32[1,256]{1,0:T(1,128)} %bitcast.9, f32[4,16384]{1,0:T(4,128)} %wx_in.1, ...), custom_call_target="tpu_custom_call" | custom-call | flops 8999999488 | bytes 18874368 | tf_op jit(solution)/shard_map/pallas_call | solution.py:457
  156.8 6.4 %shard_map.101 = bf16[4096,1024]{1,0:T(8,128)(2,1)} custom-call(bf16[4096,1024]{1,0:T(8,128)(2,1)} %shard_map.100.y_ref), custom_call_target="tpu_custom_call" | custom-call | bytes 16777216 | tf_op jit(solution)/shard_map/pallas_call | solution.py:534

commit v7 on v6

--- a/solution.py
+++ b/solution.py
@@ -374,8 +374,11 @@
             incoming_pass(p - 1)
     incoming_pass(PIECES - 1)
 
-    def out_copy(j):
-        return pltpu.make_async_copy(xs.at[block(j)], out_ref.at[block(j)], osem.at[j])
+    def out_copy(j, half):
+        at = pl.ds(half * (CH // 2), CH // 2)
+        return pltpu.make_async_copy(
+            xs.at[block(j), at], out_ref.at[block(j), at], osem.at[half, j]
+        )
 
     @pl.loop(0, N_INNER)
     def _(i):
@@ -392,11 +395,13 @@
             acc = acc * dot(coef[block(j), :], ee[:, lanes])
             y = acc + skip[:, lanes] * xbuf[block(j), lanes].astype(F32)
             xs[block(j), lanes] = y.astype(BF16)
-        out_copy(j).start()
+            if (q + 256) % (CH // 2) == 0:
+                out_copy(j, q // (CH // 2)).start()
 
     @pl.loop(0, N_INNER)
     def _(j):
-        out_copy(j).wait()
+        out_copy(j, 0).wait()
+        out_copy(j, 1).wait()
 
     for n in range(N_PEER):
         bc_copy(n, 0).wait_send()
@@ -511,7 +516,7 @@
             dma((N_SLAB,)),
             dma((PIECES, N_SLAB)),
             dma((PIECES, N_SLAB)),
-            dma((N_INNER,)),
+            dma((2, N_INNER)),
         ],
         compiler_params=pltpu.CompilerParams(
             collective_id=0, has_side_effects=True, vmem_limit_bytes=58 * 2**20

time: 166 us -> 166 us (level)
  no operation moved by 1% of the time
where the time goes in v7:
time: 166 us; the launch traced here: 163 us
  Pallas kernels  163 us (98%)
    pallas_call x1, Pallas kernels, shards(): pl.pallas_call(body, out_shape=jax.ShapeDtypeStruct((tok_slab, CH), BF16)...  157 us
    pallas_call x1, Pallas kernels, shards(): pl.pallas_call(hand_over, out_shape=jax.ShapeDtypeStruct((tok_slab, CH),...  6.43 us

profile of v7, /device:TPU:24, one launch (start us, length us, event | category | flops | bytes accessed | tf_op | source)
XLA Modules:
  0.0 163.2 jit_solution(12370305235430311967)
XLA Ops:
  0.0 156.8 %shard_map.100.y_ref = bf16[4096,1024]{1,0:T(8,128)(2,1)} custom-call(bf16[256,16384]{1,0:T(8,128)(2,1)} %x_ref.1, bf16[256,4096]{1,0:T(8,128)(2,1)} %bc_ref.1, bf16[256,256]{1,0:T(8,128)(2,1)} %dt_in.1, f32[1,256]{1,0:T(1,128)} %bitcast.7, f32[1,256]{1,0:T(1,128)} %bitcast.8, f32[1,256]{1,0:T(1,128)} %bitcast.9, f32[4,16384]{1,0:T(4,128)} %wx_in.1, ...), custom_call_target="tpu_custom_call" | custom-call | flops 8999999488 | bytes 18874368 | tf_op jit(solution)/shard_map/pallas_call | solution.py:462
  156.8 6.4 %shard_map.101 = bf16[4096,1024]{1,0:T(8,128)(2,1)} custom-call(bf16[4096,1024]{1,0:T(8,128)(2,1)} %shard_map.100.y_ref), custom_call_target="tpu_custom_call" | custom-call | bytes 16777216 | tf_op jit(solution)/shard_map/pallas_call | solution.py:539
